TPU v7x, 128 devices: a whole 4x4x4 slice. The times are simulated.
128 devices in a mesh: seq: 32 (over y, x, core), batch: 4 (over z).
Axes of the slice: x: 4, y: 4, z: 4, core: 2. Of those that a mesh axis runs over, the one named last changes fastest.
Arguments:
- tokens: bfloat16 [4, 16384, 768], P('batch', 'seq'), may hold values from -6 to 6
- lengths: int32 [4], P('batch'), may hold values from 8192 to 16384, as said below
- w_query: bfloat16 [768, 768], replicated, may hold values from -0.21875 to 0.21875
- b_query: float32 [768], replicated, may hold values from -3 to 3
- w_key: bfloat16 [768, 768], replicated, may hold values from -0.21875 to 0.21875
- b_key: float32 [768], replicated, may hold values from -3 to 3
- w_value: bfloat16 [768, 768], replicated, may hold values from -0.21875 to 0.21875
- b_value: float32 [768], replicated, may hold values from -0.3125 to 0.3125
- w_out: bfloat16 [768, 768], replicated, may hold values from -3 to 3
- b_out: float32 [768], replicated, may hold values from -1.75 to 1.75
- gain_one: float32 [768], replicated, may hold values from 0.1 to 1.9
- shift_one: float32 [768], replicated, may hold values from -1.75 to 1.75
- w_up: bfloat16 [768, 3072], replicated, may hold values from -0.21875 to 0.21875
- b_up: float32 [3072], replicated, may hold values from -1.75 to 1.75
- w_down: bfloat16 [3072, 768], replicated, may hold values from -0.109375 to 0.109375
- b_down: float32 [768], replicated, may hold values from -1.75 to 1.75
- gain_two: float32 [768], replicated, may hold values from 0.1 to 1.9
- shift_two: float32 [768], replicated, may hold values from -1.75 to 1.75
- cotangent: bfloat16 [4, 16384, 768], P('batch', 'seq'), may hold values from -6 to 6
Outputs:
- block_out: bfloat16 [4, 16384, 768], P('batch', 'seq')
- grad_tokens: float32 [4, 16384, 768], P('batch', 'seq')
- grad_w_query: float32 [768, 768], P('seq')
- grad_b_query: float32 [768], P('seq')
- grad_w_key: float32 [768, 768], P('seq')
- grad_b_key: float32 [768], P('seq')
- grad_w_value: float32 [768, 768], P('seq')
- grad_b_value: float32 [768], P('seq')
- grad_w_out: float32 [768, 768], P('seq')
- grad_b_out: float32 [768], P('seq')
- grad_gain_one: float32 [768], P('seq')
- grad_shift_one: float32 [768], P('seq')
- grad_w_up: float32 [768, 3072], P('seq')
- grad_b_up: float32 [3072], P('seq')
- grad_w_down: float32 [3072, 768], P('seq')
- grad_b_down: float32 [768], P('seq')
- grad_gain_two: float32 [768], P('seq')
- grad_shift_two: float32 [768], P('seq')
Inputs may be any that keep to these rules, and one draw needn't show every extreme that they name: `lengths`: in every draw one sequence has all 16384 positions real and another has exactly 8192.
All inputs are finite; a program needn't handle non-finite values.
Results may differ from a plain program's by a relative error of at most 0.012.
Values sent between devices are 32-bit elements; how exact they have to be, the bound alone decides.
A program may use at most 192 MiB of HBM per device.

v0:
```python
import jax
import jax.numpy as jnp
from jax import lax
from jax.experimental import pallas as pl
from jax.experimental.pallas import tpu as pltpu
from jax.sharding import Mesh
from jax.sharding import PartitionSpec as P

SEQ = ("seq_0", "seq_1", "seq_2")
AX = ("seq_0", "seq_1", "batch")
CORE = "seq_2"
MESH = pl.DeviceIdType.MESH
DIRECT = (1, 3, 2)
F32 = jnp.float32
BF16 = jnp.bfloat16
HALF_PI = 1.5707963267948966
HALF_PI_REST = -4.371139000186241e-08
EPSILON = 1e-05
ROWS = 512
WIDTH = 768
HIDDEN = 3072
HEADS = 12
PAIRS = 6
CHUNK = 256
TILE = 512
VMEM = pltpu.VMEM
LIMIT = 60 * 2**20


def nn(a, b):
    return jnp.dot(a, b, preferred_element_type=F32)


def nt(a, b):
    return lax.dot_general(a, b, (((1,), (1,)), ((), ())), preferred_element_type=F32)


def tn(a, b):
    return lax.dot_general(a, b, (((0,), (0,)), ((), ())), preferred_element_type=F32)


def at(k, size):
    return pl.ds(pl.multiple_of(k * size, size), size)


def rot(k, d):
    return lax.rem(k + d, 4)


def left_lanes(rows):
    return lax.broadcasted_iota(jnp.int32, (rows, 128), 1) < 64


def swap_halves(value):
    return pltpu.roll(value, 64, 1)


def doubled(value):
    return jnp.concatenate([value, value], axis=1)


def halves(value):
    high = value.astype(BF16)
    return high, (value - high.astype(F32)).astype(BF16)


SIN = (1.0, -0.1666666716337204, 0.008333330973982811, -0.00019840864115394652, 2.7525297809916083e-06, -2.3888299338636898e-08)


def sine(x):
    square = x * x
    value = SIN[5]
    for c in SIN[4::-1]:
        value = value * square + c
    return value * x


ERFCX = (
    0.22567586600780487, 0.2256695181131363, 0.2078438699245453, 0.1685338169336319, 0.14146119356155396,
    -0.005668365862220526, 0.16915558278560638, -0.18294405937194824, 0.05027270317077637,
)


def normal_parts(p):
    bell = jnp.exp(-0.5 * p * p)
    t = 1.0 / (1.0 + (0.4 * 0.7071067811865476) * jnp.abs(p))
    value = 0.5 * ERFCX[8]
    for c in ERFCX[7::-1]:
        value = value * t + 0.5 * c
    tail = value * t * bell
    return jnp.where(p >= 0, 1.0 - tail, tail), 0.3989422804014327 * bell


def trig_block(first, rows, length):
    position = first + lax.broadcasted_iota(jnp.int32, (rows, 128), 0)
    size = lax.broadcast_in_dim(length, (rows, 128), ()).astype(F32)
    angle = HALF_PI * jnp.minimum(position + 1, length).astype(F32) / size
    both = sine(jnp.where(left_lanes(rows), (HALF_PI - angle) + HALF_PI_REST, angle))
    return both, (position < length).astype(F32)


def project_kernel(start_ref, len_ref, x_ref, wq, bq, wk, bk, wv, bv,
                   q_ref, k_ref, v_ref, gate_q, gate_k, trig_ref, valid_ref, state_ref, early_ref):
    length = len_ref[0]
    start = start_ref[0]

    def angles(r, carry):
        both, valid = trig_block(start + 128 * r, 128, length)
        trig_ref[at(r, 128)] = both
        valid_ref[at(r, 128)] = both * valid
        return carry

    lax.fori_loop(0, ROWS // 128, angles, 0)
    left = left_lanes(ROWS)

    def columns(n, carry):
        cols = at(n, 256)
        x = x_ref[...]
        for w, b, out, gate, table in ((wq, bq, q_ref, gate_q, trig_ref), (wk, bk, k_ref, gate_k, valid_ref)):
            u = nn(x, w[:, cols]) + b[:, cols]
            small = jnp.exp(-jnp.abs(u))
            soft = jnp.maximum(u, 0.0) + jnp.log1p(small)
            gate[:, cols] = (jnp.where(u >= 0, 1.0, small) / (1.0 + small)).astype(BF16)
            trig = table[...]
            for j in range(2):
                part = soft[:, 128 * j : 128 * j + 128]
                other = swap_halves(part)
                out[4 * n + 2 * j] = (jnp.where(left, part, other) * trig).astype(BF16)
                out[4 * n + 2 * j + 1] = (jnp.where(left, other, part) * trig).astype(BF16)
        u = (nn(x, wv[:, cols]) + bv[:, cols]).astype(BF16).astype(F32)
        for j in range(2):
            part = u[:, 128 * j : 128 * j + 128]
            v_ref[4 * n + 2 * j] = jnp.where(left, part, 1.0).astype(BF16)
            v_ref[4 * n + 2 * j + 1] = jnp.where(left, swap_halves(part), 1.0).astype(BF16)
        return carry

    lax.fori_loop(0, WIDTH // 256, columns, 0)

    def states(p, carry):
        for j in range(2):
            h = 2 * p + j
            early = tn(v_ref[h, 0:CHUNK], k_ref[h, 0:CHUNK])
            early_ref[h] = early
            both = early + tn(v_ref[h, CHUNK:ROWS], k_ref[h, CHUNK:ROWS])
            state_ref[p, 64 * j : 64 * j + 64] = both[0:64]
            state_ref[p, 128 + j : 129 + j] = both[64:65]
        state_ref[p, 130:136] = jnp.zeros((6, 128), F32)
        return carry

    lax.fori_loop(0, PAIRS, states, 0)


def exchange_steps(pay, out, core_in, chip, give, head, tail, total, msgs, xa, ya, yb, xb, send, recv, reverse):
    my, mx = lax.axis_index("seq_0"), lax.axis_index("seq_1")
    core = lax.axis_index(CORE)
    other = 1 - core
    moves = []

    def remote(src, dst, k, target):
        copy = pltpu.make_async_remote_copy(
            src_ref=src, dst_ref=dst, send_sem=send.at[k], recv_sem=recv.at[k],
            device_id=target, device_id_type=MESH)
        copy.start()
        moves.append(copy)
        return copy

    def counts(theirs, mine):
        return theirs > mine if reverse else theirs < mine

    def chosen(flag, value):
        return jnp.where(flag, value, jnp.zeros_like(value))

    def first():
        return remote(pay.at[pl.ds(3 * other, 3)], core_in, 0, {CORE: other})

    def second(copy):
        copy.wait_recv()
        for p in range(3):
            chip[p] = pay[3 * core + p] + core_in[p]
        a = [remote(chip.at[:, pl.ds(0, 72)], xa.at[k], 1 + k, {"seq_1": rot(mx, d)}) for k, d in enumerate(DIRECT)]
        b = [remote(chip.at[:, pl.ds(72, 64)], yb.at[k], 4 + k, {"seq_0": rot(my, d)}) for k, d in enumerate(DIRECT)]
        return a, b

    def third(copies):
        a, b = copies
        for copy in a:
            copy.wait_recv()
        for p in range(3):
            some = jnp.zeros((72, 128), F32)
            every = chip[p, 0:72]
            for k, d in enumerate(DIRECT):
                piece = xa[k, p]
                some = some + chosen(counts(rot(mx, 4 - d), mx), piece)
                every = every + piece
            head[p] = some
            total[p] = every
        a = [remote(total, ya.at[k], 7 + k, {"seq_0": rot(my, d)}) for k, d in enumerate(DIRECT)]
        for copy in b:
            copy.wait_recv()
        for p in range(3):
            some = jnp.zeros((64, 128), F32)
            for k, d in enumerate(DIRECT):
                some = some + chosen(counts(rot(my, 4 - d), my), yb[k, p])
            tail[p] = some
            own = chip[p, 72:136]
            for k, d in enumerate(DIRECT):
                msgs[k, p] = some + chosen(counts(mx, rot(mx, d)), own)
        b = [remote(msgs.at[k], xb.at[k], 10 + k, {"seq_1": rot(mx, d)}) for k, d in enumerate(DIRECT)]
        return a, b

    def fourth(copies):
        a, b = copies
        for copy in a:
            copy.wait_recv()
        for copy in b:
            copy.wait_recv()
        mine = core == (0 if reverse else 1)
        for p in range(3):
            low, high = head[p], tail[p]
            for k, d in enumerate(DIRECT):
                low = low + chosen(counts(rot(my, 4 - d), my), ya[k, p])
                high = high + xb[k, p]
            own = 3 * core + p
            out[own, 0:72] = low + chosen(mine, core_in[p, 0:72])
            out[own, 72:136] = high + chosen(mine, core_in[p, 72:136])
            give[p, 0:72] = low + chosen(jnp.logical_not(mine), pay[own, 0:72])
            give[p, 72:136] = high + chosen(jnp.logical_not(mine), pay[own, 72:136])
        return remote(give, out.at[pl.ds(3 * core, 3)], 13, {CORE: other})

    def fifth(copy):
        copy.wait_recv()
        for move in moves:
            move.wait_send()

    return first, second, third, fourth, fifth


EXCHANGE_SCRATCH = [
    VMEM((3, 136, 128), F32),
    VMEM((3, 136, 128), F32),
    VMEM((3, 136, 128), F32),
    VMEM((3, 72, 128), F32),
    VMEM((3, 64, 128), F32),
    VMEM((3, 72, 128), F32),
    VMEM((3, 3, 64, 128), F32),
    VMEM((3, 3, 72, 128), F32),
    VMEM((3, 3, 72, 128), F32),
    VMEM((3, 3, 64, 128), F32),
    VMEM((3, 3, 64, 128), F32),
    pltpu.SemaphoreType.DMA((14,)),
    pltpu.SemaphoreType.DMA((14,)),
]


def greet(axes):
    barrier = pltpu.get_barrier_semaphore()
    core = lax.axis_index(CORE)
    pl.semaphore_signal(barrier, inc=1, device_id={CORE: 1 - core}, device_id_type=MESH)
    for axis in axes:
        mine = lax.axis_index(axis)
        for d in DIRECT:
            pl.semaphore_signal(barrier, inc=1, device_id={axis: rot(mine, d)}, device_id_type=MESH)
    pl.semaphore_wait(barrier, 1 + 3 * len(axes))


def exchange_kernel(reverse, pay, out, *scratch):
    greet(("seq_0", "seq_1"))
    first, second, third, fourth, fifth = exchange_steps(pay, out, *scratch, reverse)
    fifth(fourth(third(second(first()))))


def exchange(pay, reverse):
    def kernel(*refs):
        exchange_kernel(reverse, *refs)

    vmem = pl.BlockSpec(memory_space=VMEM)
    return pl.pallas_call(
        kernel,
        out_shape=jax.ShapeDtypeStruct((PAIRS, 136, 128), F32),
        in_specs=[vmem],
        out_specs=vmem,
        scratch_shapes=EXCHANGE_SCRATCH,
        compiler_params=pltpu.CompilerParams(
            collective_id=1 if reverse else 2, has_side_effects=True, vmem_limit_bytes=LIMIT),
    )(pay)


def causal_masks():
    row = lax.broadcasted_iota(jnp.int32, (CHUNK, CHUNK), 0)
    col = lax.broadcasted_iota(jnp.int32, (CHUNK, CHUNK), 1)
    return row >= col, row <= col


def prefix_state(before, p, j):
    body = before[p, 64 * j : 64 * j + 64]
    return jnp.concatenate([body, jnp.broadcast_to(before[p, 128 + j : 129 + j], (64, 128))], axis=0)


def attend(p, q_ref, k_ref, v_ref, early_ref, before, ratio_ref, inverse_ref, mixed_ref):
    causal, _ = causal_masks()
    left = left_lanes(CHUNK)
    cols = at(p, 128)
    for c in range(2):
        rows = slice(CHUNK * c, CHUNK * c + CHUNK)
        sums = []
        for j in range(2):
            h = 2 * p + j
            q, k, v = q_ref[h, rows], k_ref[h, rows], v_ref[h, rows]
            weight = jnp.where(causal, nt(q, k), 0.0).astype(BF16)
            state = prefix_state(before, p, j)
            if c == 1:
                state = state + early_ref[h]
            high, low = halves(state)
            sums.append(nn(weight, v) + nt(doubled(q), jnp.concatenate([high, low], axis=1)))
        even, odd = sums
        top = jnp.where(left, even, swap_halves(odd))
        inverse = 1.0 / jnp.where(left, swap_halves(even), odd)
        ratio = top * inverse
        ratio_ref[rows, cols] = ratio
        inverse_ref[rows, cols] = inverse
        mixed_ref[rows, cols] = ratio.astype(BF16)


def mean_rows(value):
    return jnp.mean(value, axis=-1, keepdims=True)


def standard(hidden):
    centred = hidden - mean_rows(hidden)
    scale = lax.rsqrt(mean_rows(centred * centred) + EPSILON)
    return centred * scale, scale


def norm_back(grad, normal, scale, gain):
    scaled = grad * gain
    return scale * (scaled - mean_rows(scaled) - normal * mean_rows(scaled * normal))


def column(value):
    return jnp.sum(value, axis=0, keepdims=True)


def middle_kernel(x_ref, cot_ref, q_ref, k_ref, v_ref, early_ref, before,
                  wo, bo, gain1, shift1, wup, bup, wdown, bdown, gain2, shift2,
                  block_ref, gone_ref, gn_ref, ratio_ref, after_state, late_ref,
                  gw_down, gw_up, gw_out, vec_ref,
                  inverse_ref, mixed_ref, normal_ref, scale_ref, normed_ref, acc_ref, act_ref, slope_ref,
                  gffn_ref, gproj_ref, tile_a, tile_b, store_sem):
    def per_pair(p, carry):
        attend(p, q_ref, k_ref, v_ref, early_ref, before, ratio_ref, inverse_ref, mixed_ref)
        return carry

    lax.fori_loop(0, PAIRS, per_pair, 0)
    vec_ref[...] = jnp.zeros_like(vec_ref)

    def note(k, value):
        vec_ref[k : k + 1, :] += value

    def first_norm(r, carry):
        rows = at(r, 128)
        hidden = x_ref[rows].astype(F32) + (nn(mixed_ref[rows], wo[...]) + bo[...])
        normal, scale = standard(hidden)
        normal_ref[rows] = normal
        scale_ref[rows] = jnp.broadcast_to(scale, (128, 128))
        normed_ref[rows] = (normal * gain1[...] + shift1[...]).astype(BF16)
        return carry

    lax.fori_loop(0, ROWS // 128, first_norm, 0)

    def feed(t, carry):
        cols = at(t, TILE)
        for r in range(2):
            rows = slice(CHUNK * r, CHUNK * r + CHUNK)
            pre = nn(normed_ref[rows], wup[:, cols]) + bup[:, cols]
            whole, bell = normal_parts(pre)
            act = (pre * whole).astype(BF16)
            act_ref[rows, cols] = act
            slope_ref[rows, cols] = (whole + pre * bell).astype(BF16)
            part = nn(act, wdown[cols])
            acc_ref[rows] = part + jnp.where(t == 0, 0.0, acc_ref[rows])
        return carry

    lax.fori_loop(0, HIDDEN // TILE, feed, 0)

    def second_norm(r, carry):
        rows = at(r, 128)
        hidden = normed_ref[rows].astype(F32) + (acc_ref[rows] + bdown[...])
        normal, scale = standard(hidden)
        block_ref[rows] = (normal * gain2[...] + shift2[...]).astype(BF16)
        grad = cot_ref[rows].astype(F32)
        note(7, column(grad * normal))
        note(8, column(grad))
        back = norm_back(grad, normal, scale, gain2[...])
        acc_ref[rows] = back
        low = back.astype(BF16)
        gffn_ref[rows] = low
        note(6, column(low.astype(F32)))
        return carry

    lax.fori_loop(0, ROWS // 128, second_norm, 0)

    def stores(t, slot):
        cols = at(t, TILE)
        return (pltpu.make_async_copy(tile_a.at[slot], gw_down.at[cols], store_sem.at[0, slot]),
                pltpu.make_async_copy(tile_b.at[slot], gw_up.at[:, cols], store_sem.at[1, slot]))

    def feed_back(t, carry):
        cols = at(t, TILE)
        slot = lax.rem(t, 2)

        @pl.when(t >= 2)
        def _():
            for copy in stores(t - 2, slot):
                copy.wait()

        gffn = gffn_ref[...]
        gpre = (nt(gffn, wdown[cols]) * slope_ref[:, cols].astype(F32)).astype(BF16)
        total = column(gpre.astype(F32))
        vec_ref[pl.ds(9 + t, 1), 0:TILE] = total
        tile_a[slot] = tn(act_ref[:, cols], gffn)
        tile_b[slot] = tn(normed_ref[...], gpre)
        acc_ref[...] += nt(gpre, wup[:, cols])
        for copy in stores(t, slot):
            copy.start()
        return carry

    tiles = HIDDEN // TILE
    lax.fori_loop(0, tiles, feed_back, 0)

    def first_back(r, carry):
        rows = at(r, 128)
        normal = normal_ref[rows]
        scale = scale_ref[rows, 0:1]
        grad = acc_ref[rows]
        note(4, column(grad * normal))
        note(5, column(grad))
        back = norm_back(grad, normal, scale, gain1[...])
        gone_ref[rows] = back
        low = back.astype(BF16)
        gproj_ref[rows] = low
        note(3, column(low.astype(F32)))
        acc_ref[rows] = nt(low, wo[...])
        return carry

    lax.fori_loop(0, ROWS // 128, first_back, 0)
    gw_out[...] = tn(mixed_ref[...], gproj_ref[...])

    def heads_back(p, carry):
        cols = at(p, 128)
        lane = lax.broadcasted_iota(jnp.int32, (ROWS, 128), 1)
        left = lane < 64
        gnum = (acc_ref[:, cols] * inverse_ref[:, cols]).astype(BF16).astype(F32)
        product = gnum * ratio_ref[:, cols]
        for j in range(2):
            mine = jnp.where(left, product, 0.0) if j == 0 else jnp.where(left, 0.0, product)
            gden = jnp.broadcast_to(-jnp.sum(mine, axis=1, keepdims=True), (ROWS, 128))
            high = gden.astype(BF16).astype(F32)
            ends = jnp.where(lane == 64, high, jnp.where(lane == 65, gden - high, 0.0))
            grad = jnp.where(left, gnum if j == 0 else swap_halves(gnum), ends).astype(BF16)
            gn_ref[2 * p + j] = grad
            late = tn(grad[CHUNK:ROWS], q_ref[2 * p + j, CHUNK:ROWS])
            late_ref[2 * p + j] = late
            both = late + tn(grad[0:CHUNK], q_ref[2 * p + j, 0:CHUNK])
            after_state[p, 64 * j : 64 * j + 64] = both[0:64]
            after_state[p, 128 + j : 129 + j] = both[64:65] + both[65:66]
        after_state[p, 130:136] = jnp.zeros((6, 128), F32)
        return carry

    lax.fori_loop(0, PAIRS, heads_back, 0)
    for t in (tiles - 2, tiles - 1):
        for copy in stores(t, t % 2):
            copy.wait()


ORDERS = ((1, 0, 2), (0, 2, 1), (2, 1, 0))
SUBS = 9
COLS = 256


def cell(ref, order, picks):
    at = [slice(None)] * 3
    for axis, pick in zip(order, picks):
        at[axis] = pick
    return ref.at[tuple(at)]


def halved(ref, order, pick, half):
    at = [slice(None)] * 3
    at[order[0]] = pick
    at[1 if order[0] == 0 else 0] = half
    return ref.at[tuple(at)]


def add_blocks(dst, srcs, lead):
    total = 1
    for n in lead:
        total *= n

    def step(k, carry):
        at, rest = [], k
        for n in reversed(lead):
            at.append(lax.rem(rest, n))
            rest = rest // n
        at = tuple(reversed(at))
        value = dst[at]
        for src in srcs:
            value = value + src[at]
        dst[at] = value
        return carry

    lax.fori_loop(0, total, step, 0)


def reduce_kernel(
    down, up, w_o, w_q, w_k, w_v, vec,
    out_down, out_up, out_o, out_q, out_k, out_v, out_vec,
    own, core_in, first, second, third, done, vecs,
    load_sem, core_send, core_recv, send, recv, vsend, vrecv,
):
    me = tuple(lax.axis_index(a) for a in AX)
    core = lax.axis_index(CORE)
    other = 1 - core
    barrier = pltpu.get_barrier_semaphore()
    pl.semaphore_signal(barrier, inc=1, device_id={CORE: other}, device_id_type=MESH)
    for axis in range(3):
        for d in DIRECT:
            pl.semaphore_signal(barrier, inc=1, device_id={AX[axis]: rot(me[axis], d)}, device_id_type=MESH)
    pl.semaphore_wait(barrier, 10)

    def source(s, b, half):
        columns = pl.ds(COLS * (s % 3), COLS)
        if s < 3:
            return down.at[:, :, half, b, :, columns]
        if s < 6:
            return up.at[:, :, half, :, pl.ds(768 * b + COLS * (s % 3), COLS)]
        return (w_o, w_q, w_k, w_v)[b].at[:, :, half, :, columns]

    loads, swaps, moves = {}, {}, []
    for s in (0, 4, 8, 3, 7, 2, 6, 1, 5):
        for b in range(4):
            swap = pltpu.make_async_remote_copy(
                src_ref=source(s, b, other), dst_ref=core_in.at[s, :, :, b],
                send_sem=core_send.at[s, b], recv_sem=core_recv.at[s, b],
                device_id={CORE: other}, device_id_type=MESH)
            swap.start()
            load = pltpu.make_async_copy(source(s, b, core), own.at[s, :, :, b], load_sem.at[s, b])
            load.start()
            loads[s, b], swaps[s, b] = load, swap

    def remote(src, dst, s, k, axis, d):
        copy = pltpu.make_async_remote_copy(
            src_ref=src, dst_ref=dst, send_sem=send.at[s, k], recv_sem=recv.at[s, k],
            device_id={AX[axis]: rot(me[axis], d)}, device_id_type=MESH)
        copy.start()
        moves.append(copy)
        return copy

    flight = {}

    def begin(s):
        order = ORDERS[s % 3]
        i = me[order[0]]
        mine, inbox = own.at[s], first.at[s]
        for b in range(4):
            loads[s, b].wait()
            swaps[s, b].wait_recv()
        add_blocks(mine, [core_in.at[s]], (4, 4, 4))
        lo, hi = pl.ds(0, 2), pl.ds(2, 2)
        far = rot(i, 2)
        ax = order[0]
        flight[s, "a"] = (
            remote(halved(mine, order, far, lo), inbox.at[0, pl.ds(0, 2)], s, 0, ax, 1),
            remote(halved(mine, order, far, hi), inbox.at[0, pl.ds(2, 2)], s, 1, ax, 3),
        )
        flight[s, "b"] = (
            remote(halved(mine, order, rot(i, 1), hi), inbox.at[1, pl.ds(2, 2)], s, 2, ax, 1),
            remote(halved(mine, order, rot(i, 3), lo), inbox.at[2, pl.ds(0, 2)], s, 3, ax, 3),
        )

    def relay(s):
        order = ORDERS[s % 3]
        i = me[order[0]]
        mine, inbox = own.at[s], first.at[s]
        lo, hi = pl.ds(0, 2), pl.ds(2, 2)
        ax = order[0]
        flight[s, "a"][0].wait_recv()
        part = halved(mine, order, rot(i, 1), lo)
        add_blocks(part, [inbox.at[0, pl.ds(0, 2)]], (2, 4))
        c0 = remote(part, inbox.at[1, pl.ds(0, 2)], s, 4, ax, 1)
        flight[s, "a"][1].wait_recv()
        part = halved(mine, order, rot(i, 3), hi)
        add_blocks(part, [inbox.at[0, pl.ds(2, 2)]], (2, 4))
        c1 = remote(part, inbox.at[2, pl.ds(2, 2)], s, 5, ax, 3)
        flight[s, "b"] += (c0, c1)

    def middle(s):
        order = ORDERS[s % 3]
        mine = own.at[s]
        for copy in flight[s, "b"]:
            copy.wait_recv()
        i = me[order[0]]
        add_blocks(cell(mine, order, (i,)), [first.at[s, 1], first.at[s, 2]], (4, 4))
        ax = order[1]
        flight[s, 2] = [
            remote(cell(mine, order, (i, rot(me[ax], d))), second.at[s, k], s, 6 + k, ax, d)
            for k, d in enumerate(DIRECT)
        ]

    def last(s):
        order = ORDERS[s % 3]
        mine = own.at[s]
        for copy in flight[s, 2]:
            copy.wait_recv()
        at = (me[order[0]], me[order[1]])
        add_blocks(cell(mine, order, at), [second.at[s, k] for k in range(3)], (4,))
        ax = order[2]
        flight[s, 3] = [
            remote(cell(mine, order, (*at, rot(me[ax], d))), third.at[s, k], s, 9 + k, ax, d)
            for k, d in enumerate(DIRECT)
        ]

    def spread(s):
        for copy in flight[s, 3]:
            copy.wait_recv()
        done[s, me[2]] = own[s, me[0], me[1], me[2]] + third[s, 0] + third[s, 1] + third[s, 2]
        flight[s, 4] = [
            remote(done.at[s, me[2]], done.at[s, me[2]], s, 12 + k, 2, d)
            for k, d in enumerate(DIRECT)
        ]

    def finish(s):
        for copy in flight[s, 4]:
            copy.wait_recv()
        c = pl.ds(COLS * (s % 3), COLS)
        for b in range(4):
            if s < 3:
                out_down[24 * b : 24 * b + 24, c] = done[s, b]
            elif s < 6:
                out_up[:, pl.ds(768 * b + COLS * (s % 3), COLS)] = done[s, b]
            else:
                (out_o, out_q, out_k, out_v)[b][:, c] = done[s, b]

    vecs[0] = vec[...]
    vmoves = {}

    def vector_send(stage):
        if stage == 0:
            targets = [{CORE: other}]
        else:
            ax = stage - 1
            targets = [{AX[ax]: rot(me[ax], d)} for d in DIRECT]
        base = (0, 1, 4, 7)[stage]
        vmoves[stage] = []
        for k, target in enumerate(targets):
            copy = pltpu.make_async_remote_copy(
                src_ref=vecs.at[stage], dst_ref=vecs.at[5 + base + k],
                send_sem=vsend.at[base + k], recv_sem=vrecv.at[base + k],
                device_id=target, device_id_type=MESH)
            copy.start()
            vmoves[stage].append(copy)

    def vector_sum(stage):
        base = (0, 1, 4, 7)[stage]
        total = vecs[stage]
        for k, copy in enumerate(vmoves[stage]):
            copy.wait_recv()
            total = total + vecs[5 + base + k]
        vecs[stage + 1] = total

    G = [(0, 4, 8), (3, 7, 2), (6, 1, 5)]

    def run(step, g):
        for s in G[g]:
            step(s)

    vector_send(0)
    run(begin, 0)
    vector_sum(0)
    vector_send(1)
    run(relay, 0)
    run(begin, 1)
    run(middle, 0)
    vector_sum(1)
    vector_send(2)
    run(relay, 1)
    run(begin, 2)
    run(last, 0)
    run(middle, 1)
    run(relay, 2)
    run(spread, 0)
    vector_sum(2)
    vector_send(3)
    run(last, 1)
    run(middle, 2)
    run(finish, 0)
    run(spread, 1)
    run(last, 2)
    vector_sum(3)
    out_vec[...] = vecs[4]
    run(finish, 1)
    run(spread, 2)
    run(finish, 2)
    for copy in [*moves, *swaps.values(), *(c for cs in vmoves.values() for c in cs)]:
        copy.wait_send()


def reduce_grads(down, up, w_o, w_q, w_k, w_v, vec):
    f32 = jnp.float32
    shapes = [(96, 768), (24, 3072), (24, 768), (24, 768), (24, 768), (24, 768), (16, 768)]
    any_spec = pl.BlockSpec(memory_space=pl.ANY)
    vmem = pl.BlockSpec(memory_space=pltpu.VMEM)
    return pl.pallas_call(
        reduce_kernel,
        out_shape=[jax.ShapeDtypeStruct(s, f32) for s in shapes],
        in_specs=[any_spec] * 6 + [vmem],
        out_specs=[vmem] * 7,
        scratch_shapes=[
            pltpu.VMEM((SUBS, 4, 4, 4, 24, COLS), f32),
            pltpu.VMEM((SUBS, 4, 4, 4, 24, COLS), f32),
            pltpu.VMEM((SUBS, 3, 4, 4, 24, COLS), f32),
            pltpu.VMEM((SUBS, 3, 4, 24, COLS), f32),
            pltpu.VMEM((SUBS, 3, 24, COLS), f32),
            pltpu.VMEM((SUBS, 4, 24, COLS), f32),
            pltpu.VMEM((15, 16, 768), f32),
            pltpu.SemaphoreType.DMA((SUBS, 4)),
            pltpu.SemaphoreType.DMA((SUBS, 4)),
            pltpu.SemaphoreType.DMA((SUBS, 4)),
            pltpu.SemaphoreType.DMA((SUBS, 15)),
            pltpu.SemaphoreType.DMA((SUBS, 15)),
            pltpu.SemaphoreType.DMA((10,)),
            pltpu.SemaphoreType.DMA((10,)),
        ],
        compiler_params=pltpu.CompilerParams(
            collective_id=0, has_side_effects=True, vmem_limit_bytes=60 * 2**20
        ),
    )(
        down.reshape(4, 4, 2, 4, 24, 768),
        up.reshape(4, 4, 2, 24, 3072),
        *(w.reshape(4, 4, 2, 24, 768) for w in (w_o, w_q, w_k, w_v)),
        vec,
    )


def suffix_state(after, p, j):
    body = after[p, 64 * j : 64 * j + 64]
    row = jnp.broadcast_to(after[p, 128 + j : 129 + j], (64, 128))
    first = lax.broadcasted_iota(jnp.int32, (64, 128), 0) == 0
    return jnp.concatenate([body, jnp.where(first, row, 0.0)], axis=0)


def attend_back(p, q_ref, k_ref, v_ref, gn_ref, early_ref, late_ref, before, after, trig_ref, valid_ref,
                gate_q, gate_k, grad_ref):
    causal, flipped = causal_masks()
    left = left_lanes(CHUNK)
    for c in range(2):
        rows = slice(CHUNK * c, CHUNK * c + CHUNK)
        query, keys, value = [], [], []
        for j in range(2):
            h = 2 * p + j
            q, k, v, g = q_ref[h, rows], k_ref[h, rows], v_ref[h, rows], gn_ref[h, rows]
            past = prefix_state(before, p, j)
            if c == 1:
                past = past + early_ref[h]
            future = suffix_state(after, p, j)
            if c == 0:
                future = future + late_ref[h]
            past_high, past_low = halves(past)
            next_high, next_low = halves(future)
            weight = jnp.where(causal, nt(g, v), 0.0).astype(BF16)
            gq = nn(weight, k) + nn(doubled(g), jnp.concatenate([past_high, past_low], axis=0))
            weight = jnp.where(flipped, nt(v, g), 0.0).astype(BF16)
            gk = nn(weight, q) + nn(doubled(v), jnp.concatenate([next_high, next_low], axis=0))
            weight = jnp.where(flipped, nt(k, q), 0.0).astype(BF16)
            gv = nn(weight, g) + nt(doubled(k), jnp.concatenate([next_high, next_low], axis=1))
            gq = gq * trig_ref[rows]
            gk = gk * valid_ref[rows]
            query.append(gq + swap_halves(gq))
            keys.append(gk + swap_halves(gk))
            value.append(gv)
        cols = at(p, 128)
        grad_ref[0, rows, cols] = (jnp.where(left, query[0], query[1]) * gate_q[rows, cols].astype(F32)).astype(BF16)
        grad_ref[1, rows, cols] = (jnp.where(left, keys[0], keys[1]) * gate_k[rows, cols].astype(F32)).astype(BF16)
        grad_ref[2, rows, cols] = jnp.where(left, value[0], swap_halves(value[1])).astype(BF16)


def last_kernel(x_ref, q_ref, k_ref, v_ref, gn_ref, early_ref, late_ref, before, after, trig_ref, valid_ref,
                gate_q, gate_k, gone_ref, wq, wk, wv,
                tokens_ref, gw_q, gw_k, gw_v, vec_ref, grad_ref):
    def per_pair(p, carry):
        attend_back(p, q_ref, k_ref, v_ref, gn_ref, early_ref, late_ref, before, after, trig_ref, valid_ref,
                    gate_q, gate_k, grad_ref)
        return carry

    lax.fori_loop(0, PAIRS, per_pair, 0)
    vec_ref[...] = jnp.zeros_like(vec_ref)
    for i, out in enumerate((gw_q, gw_k, gw_v)):
        vec_ref[i : i + 1, :] = column(grad_ref[i].astype(F32))

        def product(n, carry):
            cols = at(n, 256)
            out[:, cols] = tn(x_ref[...], grad_ref[i, :, cols])
            return carry

        lax.fori_loop(0, WIDTH // 256, product, 0)

    def back(r, carry):
        rows = at(r, 128)
        total = gone_ref[rows]
        for i, w in enumerate((wq, wk, wv)):
            total = total + nt(grad_ref[i, rows], w[...])
        tokens_ref[rows] = total
        return carry

    lax.fori_loop(0, ROWS // 128, back, 0)


def plain_call(kernel, outs, args, specs=None, scratch=(), out_specs=None):
    vmem = pl.BlockSpec(memory_space=VMEM)
    return pl.pallas_call(
        kernel,
        out_shape=[jax.ShapeDtypeStruct(shape, dtype) for shape, dtype in outs],
        in_specs=specs or [vmem] * len(args),
        out_specs=out_specs or [vmem] * len(outs),
        scratch_shapes=list(scratch),
        compiler_params=pltpu.CompilerParams(vmem_limit_bytes=LIMIT),
    )(*args)


def on_device(tokens, lengths, w_query, b_query, w_key, b_key, w_value, b_value, w_out, b_out, gain_one, shift_one,
              w_up, b_up, w_down, b_down, gain_two, shift_two, cotangent):
    x = tokens[0]
    cot = cotangent[0]
    seq = lax.axis_index(SEQ)

    def row(v):
        return v.reshape(1, -1)

    vmem = pl.BlockSpec(memory_space=VMEM)
    smem = pl.BlockSpec(memory_space=pltpu.SMEM)
    anywhere = pl.BlockSpec(memory_space=pl.ANY)
    by_head = ((HEADS, ROWS, 128), BF16)
    wide16, wide32 = ((ROWS, WIDTH), BF16), ((ROWS, WIDTH), F32)
    table = ((ROWS, 128), F32)
    per_head = ((HEADS, 128, 128), F32)
    packed = ((PAIRS, 136, 128), F32)
    q, k, v, gate_q, gate_k, trig, valid, state, early = plain_call(
        project_kernel,
        [by_head, by_head, by_head, wide16, wide16, table, table, packed, per_head],
        [(seq * ROWS).reshape(1), lengths, x, w_query, row(b_query), w_key, row(b_key), w_value, row(b_value)],
        [smem, smem] + [vmem] * 7)
    before = exchange(state, False)
    block, gone, gn, ratio, after_state, late, gw_down, gw_up, gw_out, vec = plain_call(
        middle_kernel,
        [wide16, wide32, by_head, wide32, packed, per_head,
         ((HIDDEN, WIDTH), F32), ((WIDTH, HIDDEN), F32), ((WIDTH, WIDTH), F32), ((16, WIDTH), F32)],
        [x, cot, q, k, v, early, before, w_out, row(b_out), row(gain_one), row(shift_one),
         w_up, row(b_up), w_down, row(b_down), row(gain_two), row(shift_two)],
        scratch=[
            VMEM(*wide32), VMEM(*wide16), VMEM(*wide32), VMEM(*table), VMEM(*wide16), VMEM(*wide32),
            VMEM((ROWS, HIDDEN), BF16), VMEM((ROWS, HIDDEN), BF16), VMEM(*wide16), VMEM(*wide16),
            VMEM((2, TILE, WIDTH), F32), VMEM((2, WIDTH, TILE), F32), pltpu.SemaphoreType.DMA((2, 2))],
        out_specs=[vmem] * 6 + [anywhere, anywhere, vmem, vmem])
    after = exchange(after_state, True)
    tokens_grad, gw_q, gw_k, gw_v, vec_two = plain_call(
        last_kernel,
        [wide32] + [((WIDTH, WIDTH), F32)] * 3 + [((16, WIDTH), F32)],
        [x, q, k, v, gn, early, late, before, after, trig, valid, gate_q, gate_k, gone, w_query, w_key, w_value],
        scratch=[VMEM((3, ROWS, WIDTH), BF16)])
    sum_down, sum_up, sum_out, sum_query, sum_key, sum_value, sums = reduce_grads(
        gw_down, gw_up, gw_out, gw_q, gw_k, gw_v, vec + vec_two)
    small = lax.dynamic_slice(sums, (0, 24 * seq), (9, 24))
    wide = lax.dynamic_slice(sums[9:15, :TILE].reshape(-1), (96 * seq,), (96,))
    return (
        block[None], tokens_grad[None], sum_query, small[0], sum_key, small[1], sum_value, small[2],
        sum_out, small[3], small[4], small[5], sum_up, wide, sum_down, small[6], small[7], small[8],
    )


def solution(mesh):
    torus = Mesh(mesh.devices.reshape(4, 4, 2, mesh.shape["batch"]), (*SEQ, "batch"))
    rows, shares = P("batch", SEQ, None), P(SEQ, None)
    return jax.shard_map(
        on_device,
        mesh=torus,
        in_specs=(rows, P("batch")) + (P(),) * 16 + (rows,),
        out_specs=(rows, rows) + (shares, P(SEQ)) * 4 + (P(SEQ), P(SEQ)) + (shares, P(SEQ)) * 2 + (P(SEQ), P(SEQ)),
        check_vma=False,
    )
```

profile of v0, /device:TPU:0, one launch (start us, length us, event | category | flops | bytes accessed | tf_op | source)
XLA Modules:
  0.0 244.9 jit_solution(3277973251167052468)
XLA Ops:
  0.7 1.3 reshape.91.bq
  1.9 1.3 reshape.92.bk
  3.2 1.3 reshape.93.bv
  5.1 0.0 copy-start.1
  5.1 0.0 copy-start.2
  5.1 0.0 copy-start.3
  5.2 0.0 copy-start.4
  5.2 0.0 copy-start.5
  5.2 0.0 copy-start.6
  5.2 11.3 %shard_map.322 = (bf16[12,512,128]{2,1,0:T(8,128)(2,1)}, bf16[12,512,128]{2,1,0:T(8,128)(2,1)}, bf16[12,512,128]{2,1,0:T(8,128)(2,1)}, bf16[512,768]{1,0:T(8,128...) custom-call(s32[1]{0:T(128)} %bitcast.2.start_ref, ...), custom_call_target="tpu_custom_call" | custom-call | tf_op jit(solution)/shard_map/pallas_call | solution.py:819
  16.5 23.0 %shard_map.323.before = f32[6,136,128]{2,1,0:T(8,128)} custom-call(f32[6,136,128]{2,1,0:T(8,128)} %get-tuple-element.52.refs_0_), custom_call_target="tpu_custom_call" | custom-call | tf_op jit(solution)/shard_map/pallas_call | solution.py:277
  39.5 0.0 copy-done.1
  39.5 0.6 reshape.100.shift2
  40.1 0.0 copy-done.2
  40.1 0.6 reshape.94.bo
  40.7 0.0 copy-done.3
  40.7 0.6 reshape.95.gain1
  41.2 0.0 copy-done.4
  41.2 0.6 reshape.96.shift1
  41.8 0.0 copy-done.5
  41.8 0.6 reshape.98.bdown
  42.4 0.0 copy-done.6
  42.4 0.6 reshape.99.gain2
  43.0 48.6 %shard_map.324 = (bf16[512,768]{1,0:T(8,128)(2,1)}, f32[512,768]{1,0:T(8,128)}, bf16[12,512,128]{2,1,0:T(8,128)(2,1)}, f32[512,768]{1,0:T(8,128)}, f32[6,136,128...) custom-call(bf16[512,768]{1,0:T(8,128)(2,1)} %bitcast.33, ...), custom_call_target="tpu_custom_call" | custom-call | tf_op jit(solution)/shard_map/pallas_call | solution.py:819
  91.6 21.6 %shard_map.325.after = f32[6,136,128]{2,1,0:T(8,128)} custom-call(f32[6,136,128]{2,1,0:T(8,128)} %get-tuple-element.56.refs_0_), custom_call_target="tpu_custom_call" | custom-call | tf_op jit(solution)/shard_map/pallas_call | solution.py:277
  113.2 0.0 copy-start
  113.2 28.3 %shard_map.326 = (f32[512,768]{1,0:T(8,128)}, f32[768,768]{1,0:T(8,128)}, f32[768,768]{1,0:T(8,128)}, f32[768,768]{1,0:T(8,128)}, f32[16,768]{1,0:T(8,128)}) custom-call(bf16[512,768]{1,0:T(8,128)(2,1)} %bitcast.34, bf16[12,512,128]{2,1,0:T(8,128)(2,1)} %get-tuple-element.48.q_ref, bf16[12,512,128]{2,1,0:T(8,128)(2,1)} %get-tuple-element.49.k_ref, ...), custom_call_target="tpu_custom_call" | custom-call | tf_op jit(solution)/shard_map/pallas_call | solution.py:819
  141.5 0.0 copy-done
  141.5 1.4 add.17.vec
  142.9 89.6 %shard_map.327 = (f32[96,768]{1,0:T(8,128)}, f32[24,3072]{1,0:T(8,128)}, f32[24,768]{1,0:T(8,128)}, f32[24,768]{1,0:T(8,128)}, f32[24,768]{1,0:T(8,128)}, /*index=5*/f32[24,768]{1,0:T(8,128)}, f32[16,768]{1,0:T(8,128)}) custom-call(f32[4,4,2,4,24,768]{5,4,3,2,1,0:T(8,128)} %bitcast.30, f32[4,4,2,24,3072]{4,3,2,1,0:T(8,128)} %bitcast.31, ...), custom_call_target="tpu_custom_call" | custom-call | tf_op jit(solution)/shard_map/pallas_call | solution.py:712
  232.5 0.7 slice.36
  233.2 0.6 dynamic_slice.7
  233.8 1.6 dynamic-slice_bitcast_fusion
  235.4 1.5 copy.44
  237.0 1.5 copy.45
  238.5 1.5 copy.46
  240.0 1.5 copy.47
  241.5 1.7 copy.48
  243.2 1.7 copy.49
  (1 shorter events, 0.0 us)
Async XLA Ops:
  5.1 34.4 %copy-start.1 = (f32[768]{0:T(1024)S(1)}, f32[768]{0:T(1024)}, u32[]{:S(2)}) copy-start(f32[768]{0:T(1024)} %param.36) | copy-start | bytes 9220
  5.1 35.0 %copy-start.2 = (f32[768]{0:T(1024)S(1)}, f32[768]{0:T(1024)}, u32[]{:S(2)}) copy-start(f32[768]{0:T(1024)} %param.28) | copy-start | bytes 9220
  5.1 35.5 %copy-start.3 = (f32[768]{0:T(1024)S(1)}, f32[768]{0:T(1024)}, u32[]{:S(2)}) copy-start(f32[768]{0:T(1024)} %param.29) | copy-start | bytes 9220
  5.2 36.1 %copy-start.4 = (f32[768]{0:T(1024)S(1)}, f32[768]{0:T(1024)}, u32[]{:S(2)}) copy-start(f32[768]{0:T(1024)} %param.30) | copy-start | bytes 9220
  5.2 36.7 %copy-start.5 = (f32[768]{0:T(1024)S(1)}, f32[768]{0:T(1024)}, u32[]{:S(2)}) copy-start(f32[768]{0:T(1024)} %param.34) | copy-start | bytes 9220
  5.2 37.3 %copy-start.6 = (f32[768]{0:T(1024)S(1)}, f32[768]{0:T(1024)}, u32[]{:S(2)}) copy-start(f32[768]{0:T(1024)} %param.35) | copy-start | bytes 9220
  113.2 28.3 %copy-start = (f32[16,768]{1,0:T(8,128)S(1)}, f32[16,768]{1,0:T(8,128)}, u32[]{:S(2)}) copy-start(f32[16,768]{1,0:T(8,128)} %get-tuple-element.69) | copy-start | bytes 147460
where the time goes:
time: 246 us; the launch traced here: 245 us
  Pallas kernels  222 us (90%)
  local copies, waits for them, and re-layouts  19.7 us (8%)
    pallas_call x1, Pallas kernels, reduce_grads(): pl.pallas_call(reduce_kernel, out_shape=[jax.ShapeDtypeStruct(s, f32) for...  89.6 us
    pallas_call x3, Pallas kernels, plain_call(): pl.pallas_call(kernel, out_shape=[jax.ShapeDtypeStruct(shape, dtype) for...  88.2 us
    pallas_call x2, Pallas kernels, exchange(): pl.pallas_call(kernel, out_shape=jax.ShapeDtypeStruct((PAIRS, 136, 128),...  44.6 us
    unnamed x20, local copies, waits for them, and re-layouts  9.51 us
    reshape x9, local copies, waits for them, and re-layouts, row(): return v.reshape(1, -1)  7.3 us

commit v1 on v0

--- a/solution.py
+++ b/solution.py
@@ -99,55 +99,43 @@
     return both, (position < length).astype(F32)
 
 
-def project_kernel(start_ref, len_ref, x_ref, wq, bq, wk, bk, wv, bv,
-                   q_ref, k_ref, v_ref, gate_q, gate_k, trig_ref, valid_ref, state_ref, early_ref):
-    length = len_ref[0]
-    start = start_ref[0]
-
-    def angles(r, carry):
-        both, valid = trig_block(start + 128 * r, 128, length)
-        trig_ref[at(r, 128)] = both
-        valid_ref[at(r, 128)] = both * valid
-        return carry
-
-    lax.fori_loop(0, ROWS // 128, angles, 0)
+def project_keys(n, x_ref, wk, bk, wv, bv, qk_ref, v_ref, gate_k, valid_ref):
+    cols = at(n, 256)
     left = left_lanes(ROWS)
-
-    def columns(n, carry):
-        cols = at(n, 256)
-        x = x_ref[...]
-        for w, b, out, gate, table in ((wq, bq, q_ref, gate_q, trig_ref), (wk, bk, k_ref, gate_k, valid_ref)):
-            u = nn(x, w[:, cols]) + b[:, cols]
-            small = jnp.exp(-jnp.abs(u))
-            soft = jnp.maximum(u, 0.0) + jnp.log1p(small)
-            gate[:, cols] = (jnp.where(u >= 0, 1.0, small) / (1.0 + small)).astype(BF16)
-            trig = table[...]
-            for j in range(2):
-                part = soft[:, 128 * j : 128 * j + 128]
-                other = swap_halves(part)
-                out[4 * n + 2 * j] = (jnp.where(left, part, other) * trig).astype(BF16)
-                out[4 * n + 2 * j + 1] = (jnp.where(left, other, part) * trig).astype(BF16)
-        u = (nn(x, wv[:, cols]) + bv[:, cols]).astype(BF16).astype(F32)
-        for j in range(2):
-            part = u[:, 128 * j : 128 * j + 128]
-            v_ref[4 * n + 2 * j] = jnp.where(left, part, 1.0).astype(BF16)
-            v_ref[4 * n + 2 * j + 1] = jnp.where(left, swap_halves(part), 1.0).astype(BF16)
-        return carry
-
-    lax.fori_loop(0, WIDTH // 256, columns, 0)
-
-    def states(p, carry):
-        for j in range(2):
-            h = 2 * p + j
-            early = tn(v_ref[h, 0:CHUNK], k_ref[h, 0:CHUNK])
-            early_ref[h] = early
-            both = early + tn(v_ref[h, CHUNK:ROWS], k_ref[h, CHUNK:ROWS])
-            state_ref[p, 64 * j : 64 * j + 64] = both[0:64]
-            state_ref[p, 128 + j : 129 + j] = both[64:65]
-        state_ref[p, 130:136] = jnp.zeros((6, 128), F32)
-        return carry
-
-    lax.fori_loop(0, PAIRS, states, 0)
+    x = x_ref[...]
+    u = (nn(x, wv[:, cols]) + bv[:, cols]).astype(BF16).astype(F32)
+    for j in range(2):
+        part = u[:, 128 * j : 128 * j + 128]
+        v_ref[:, at(4 * n + 2 * j, 128)] = jnp.where(left, part, 1.0).astype(BF16)
+        v_ref[:, at(4 * n + 2 * j + 1, 128)] = jnp.where(left, swap_halves(part), 1.0).astype(BF16)
+    project_soft(n, HEADS, x, wk, bk, qk_ref, gate_k, valid_ref)
+
+
+def project_soft(n, first, x, w, b, out, gate, table):
+    cols = at(n, 256)
+    left = left_lanes(ROWS)
+    u = nn(x, w[:, cols]) + b[:, cols]
+    small = jnp.exp(-jnp.abs(u))
+    soft = jnp.maximum(u, 0.0) + jnp.log1p(small)
+    gate[:, cols] = (jnp.where(u >= 0, 1.0, small) / (1.0 + small)).astype(BF16)
+    trig = table[...]
+    for j in range(2):
+        part = soft[:, 128 * j : 128 * j + 128]
+        other = swap_halves(part)
+        out[:, at(first + 4 * n + 2 * j, 128)] = (jnp.where(left, part, other) * trig).astype(BF16)
+        out[:, at(first + 4 * n + 2 * j + 1, 128)] = (jnp.where(left, other, part) * trig).astype(BF16)
+
+
+def state_sums(p, qk_ref, v_ref, state_ref, early_ref):
+    for j in range(2):
+        h = 2 * p + j
+        keys, values = at(HEADS + h, 128), at(h, 128)
+        early = tn(v_ref[0:CHUNK, values], qk_ref[0:CHUNK, keys])
+        early_ref[h] = early
+        both = early + tn(v_ref[CHUNK:ROWS, values], qk_ref[CHUNK:ROWS, keys])
+        state_ref[p, 64 * j : 64 * j + 64] = both[0:64]
+        state_ref[p, 128 + j : 129 + j] = both[64:65]
+    state_ref[p, 130:136] = jnp.zeros((6, 128), F32)
 
 
 def exchange_steps(pay, out, core_in, chip, give, head, tail, total, msgs, xa, ya, yb, xb, send, recv, reverse):
@@ -260,11 +248,15 @@
         mine = lax.axis_index(axis)
         for d in DIRECT:
             pl.semaphore_signal(barrier, inc=1, device_id={axis: rot(mine, d)}, device_id_type=MESH)
-    pl.semaphore_wait(barrier, 1 + 3 * len(axes))
+
+
+def greeted(axes):
+    pl.semaphore_wait(pltpu.get_barrier_semaphore(), 1 + 3 * len(axes))
 
 
 def exchange_kernel(reverse, pay, out, *scratch):
     greet(("seq_0", "seq_1"))
+    greeted(("seq_0", "seq_1"))
     first, second, third, fourth, fifth = exchange_steps(pay, out, *scratch, reverse)
     fifth(fourth(third(second(first()))))
 
@@ -296,8 +288,17 @@
     return jnp.concatenate([body, jnp.broadcast_to(before[p, 128 + j : 129 + j], (64, 128))], axis=0)
 
 
-def attend(p, q_ref, k_ref, v_ref, early_ref, before, ratio_ref, inverse_ref, mixed_ref):
+def attend_local(p, qk_ref, v_ref, num_ref):
     causal, _ = causal_masks()
+    for c in range(2):
+        rows = slice(CHUNK * c, CHUNK * c + CHUNK)
+        for j in range(2):
+            h = 2 * p + j
+            weight = nt(qk_ref[rows, at(h, 128)], qk_ref[rows, at(HEADS + h, 128)])
+            num_ref[h, rows] = nn(jnp.where(causal, weight, 0.0).astype(BF16), v_ref[rows, at(h, 128)])
+
+
+def attend_earlier(p, qk_ref, num_ref, early_ref, before, ratio_ref, inverse_ref, mixed_ref):
     left = left_lanes(CHUNK)
     cols = at(p, 128)
     for c in range(2):
@@ -305,13 +306,12 @@
         sums = []
         for j in range(2):
             h = 2 * p + j
-            q, k, v = q_ref[h, rows], k_ref[h, rows], v_ref[h, rows]
-            weight = jnp.where(causal, nt(q, k), 0.0).astype(BF16)
             state = prefix_state(before, p, j)
             if c == 1:
                 state = state + early_ref[h]
             high, low = halves(state)
-            sums.append(nn(weight, v) + nt(doubled(q), jnp.concatenate([high, low], axis=1)))
+            q = qk_ref[rows, at(h, 128)]
+            sums.append(num_ref[h, rows] + nt(doubled(q), jnp.concatenate([high, low], axis=1)))
         even, odd = sums
         top = jnp.where(left, even, swap_halves(odd))
         inverse = 1.0 / jnp.where(left, swap_halves(even), odd)
@@ -340,21 +340,93 @@
     return jnp.sum(value, axis=0, keepdims=True)
 
 
-def middle_kernel(x_ref, cot_ref, q_ref, k_ref, v_ref, early_ref, before,
-                  wo, bo, gain1, shift1, wup, bup, wdown, bdown, gain2, shift2,
-                  block_ref, gone_ref, gn_ref, ratio_ref, after_state, late_ref,
-                  gw_down, gw_up, gw_out, vec_ref,
-                  inverse_ref, mixed_ref, normal_ref, scale_ref, normed_ref, acc_ref, act_ref, slope_ref,
-                  gffn_ref, gproj_ref, tile_a, tile_b, store_sem):
-    def per_pair(p, carry):
-        attend(p, q_ref, k_ref, v_ref, early_ref, before, ratio_ref, inverse_ref, mixed_ref)
-        return carry
-
-    lax.fori_loop(0, PAIRS, per_pair, 0)
+def front_kernel(len_ref, bq, bk, bv, bo, gain1, shift1, bup, bdown, gain2, shift2,
+                 x_hbm, wq_hbm, wk_hbm, wv_hbm, wo_hbm, wup_hbm, wdown_hbm, cot_hbm,
+                 qk_out, v_out, gates_out, trigs_out, early_out, before_out, ratio_out, inverse_out, mixed_out,
+                 normal_out, scale_out, normed_out, act_out, slope_out, back_out, gffn_out, block_out, vec_out,
+                 x_ref, wq, wk, wv, wo, wup, wdown, cot_ref,
+                 qk_ref, v_ref, gates, trigs, early_ref, before, ratio_ref, inverse_ref, mixed_ref,
+                 normal_ref, scale_ref, normed_ref, act_ref, slope_ref, acc_ref, gffn_ref, block_ref, vec_ref,
+                 state_ref, num_ref, load_sem, store_sem, *scratch):
+    greet(("seq_0", "seq_1"))
+    pairs = ((x_hbm, x_ref), (wk_hbm, wk), (wv_hbm, wv), (wq_hbm, wq), (wo_hbm, wo), (wup_hbm, wup),
+             (wdown_hbm, wdown), (cot_hbm, cot_ref))
+    loads = [pltpu.make_async_copy(src, dst, load_sem.at[k]) for k, (src, dst) in enumerate(pairs)]
+    for load in loads:
+        load.start()
+    stores = []
+
+    def store(src, dst):
+        copy = pltpu.make_async_copy(src, dst, store_sem.at[len(stores)])
+        copy.start()
+        stores.append(copy)
+
+    length = len_ref[0]
+    start = ROWS * ((lax.axis_index("seq_0") * 4 + lax.axis_index("seq_1")) * 2 + lax.axis_index(CORE))
+
+    def angles(r, carry):
+        both, valid = trig_block(start + 128 * r, 128, length)
+        trigs[0, at(r, 128)] = both
+        trigs[1, at(r, 128)] = both * valid
+        return carry
+
+    lax.fori_loop(0, ROWS // 128, angles, 0)
+    store(trigs, trigs_out)
+    for k in range(3):
+        loads[k].wait()
+
+    def keys(n, carry):
+        project_keys(n, x_ref, wk, bk, wv, bv, qk_ref, v_ref, gates.at[1], trigs.at[1])
+        return carry
+
+    lax.fori_loop(0, WIDTH // 256, keys, 0)
+
+    def states(p, carry):
+        state_sums(p, qk_ref, v_ref, state_ref, early_ref)
+        return carry
+
+    lax.fori_loop(0, PAIRS, states, 0)
+    store(v_ref, v_out)
+    store(early_ref, early_out)
+    greeted(("seq_0", "seq_1"))
+    first, second, third, fourth, fifth = exchange_steps(state_ref, before, *scratch, False)
+    stage = first()
+    loads[3].wait()
+
+    def queries(n, carry):
+        project_soft(n, 0, x_ref[...], wq, bq, qk_ref, gates.at[0], trigs.at[0])
+        return carry
+
+    def local(p, carry):
+        attend_local(p, qk_ref, v_ref, num_ref)
+        return carry
+
+    lax.fori_loop(0, 1, queries, 0)
+    stage = second(stage)
+    lax.fori_loop(1, WIDTH // 256, queries, 0)
+    store(qk_ref, qk_out)
+    store(gates, gates_out)
+    lax.fori_loop(0, 3, local, 0)
+    stage = third(stage)
+    lax.fori_loop(3, PAIRS, local, 0)
+    stage = fourth(stage)
+    fifth(stage)
+    store(before, before_out)
+
+    def earlier(p, carry):
+        attend_earlier(p, qk_ref, num_ref, early_ref, before, ratio_ref, inverse_ref, mixed_ref)
+        return carry
+
+    lax.fori_loop(0, PAIRS, earlier, 0)
+    store(ratio_ref, ratio_out)
+    store(inverse_ref, inverse_out)
+    store(mixed_ref, mixed_out)
     vec_ref[...] = jnp.zeros_like(vec_ref)
 
     def note(k, value):
         vec_ref[k : k + 1, :] += value
+
+    loads[4].wait()
 
     def first_norm(r, carry):
         rows = at(r, 128)
@@ -366,6 +438,11 @@
         return carry
 
     lax.fori_loop(0, ROWS // 128, first_norm, 0)
+    store(normal_ref, normal_out)
+    store(scale_ref, scale_out)
+    store(normed_ref, normed_out)
+    loads[5].wait()
+    loads[6].wait()
 
     def feed(t, carry):
         cols = at(t, TILE)
@@ -381,6 +458,9 @@
         return carry
 
     lax.fori_loop(0, HIDDEN // TILE, feed, 0)
+    store(act_ref, act_out)
+    store(slope_ref, slope_out)
+    loads[7].wait()
 
     def second_norm(r, carry):
         rows = at(r, 128)
@@ -398,6 +478,24 @@
         return carry
 
     lax.fori_loop(0, ROWS // 128, second_norm, 0)
+    store(gffn_ref, gffn_out)
+    store(acc_ref, back_out)
+    store(block_ref, block_out)
+    store(vec_ref, vec_out)
+    for copy in stores:
+        copy.wait()
+
+
+def middle_kernel(qk_ref, ratio_ref, inverse_ref, mixed_ref, normal_ref, scale_ref, normed_ref, act_ref, slope_ref,
+                  acc_ref, gffn_ref, wo, wup, gain1, wdown,
+                  gone_ref, gn_ref, after_state, late_ref, gw_down, gw_up, gw_out, vec_ref,
+                  gproj_ref, scratch_ref, tile_a, tile_b, store_sem):
+    vec_ref[...] = jnp.zeros_like(vec_ref)
+
+    def note(k, value):
+        vec_ref[k : k + 1, :] += value
+
+    gone_ref[...] = acc_ref[...]
 
     def stores(t, slot):
         cols = at(t, TILE)
@@ -419,7 +517,7 @@
         vec_ref[pl.ds(9 + t, 1), 0:TILE] = total
         tile_a[slot] = tn(act_ref[:, cols], gffn)
         tile_b[slot] = tn(normed_ref[...], gpre)
-        acc_ref[...] += nt(gpre, wup[:, cols])
+        gone_ref[...] += nt(gpre, wup[:, cols])
         for copy in stores(t, slot):
             copy.start()
         return carry
@@ -431,7 +529,7 @@
         rows = at(r, 128)
         normal = normal_ref[rows]
         scale = scale_ref[rows, 0:1]
-        grad = acc_ref[rows]
+        grad = gone_ref[rows]
         note(4, column(grad * normal))
         note(5, column(grad))
         back = norm_back(grad, normal, scale, gain1[...])
@@ -439,7 +537,7 @@
         low = back.astype(BF16)
         gproj_ref[rows] = low
         note(3, column(low.astype(F32)))
-        acc_ref[rows] = nt(low, wo[...])
+        scratch_ref[rows] = nt(low, wo[...])
         return carry
 
     lax.fori_loop(0, ROWS // 128, first_back, 0)
@@ -449,7 +547,7 @@
         cols = at(p, 128)
         lane = lax.broadcasted_iota(jnp.int32, (ROWS, 128), 1)
         left = lane < 64
-        gnum = (acc_ref[:, cols] * inverse_ref[:, cols]).astype(BF16).astype(F32)
+        gnum = (scratch_ref[:, cols] * inverse_ref[:, cols]).astype(BF16).astype(F32)
         product = gnum * ratio_ref[:, cols]
         for j in range(2):
             mine = jnp.where(left, product, 0.0) if j == 0 else jnp.where(left, 0.0, product)
@@ -457,10 +555,10 @@
             high = gden.astype(BF16).astype(F32)
             ends = jnp.where(lane == 64, high, jnp.where(lane == 65, gden - high, 0.0))
             grad = jnp.where(left, gnum if j == 0 else swap_halves(gnum), ends).astype(BF16)
-            gn_ref[2 * p + j] = grad
-            late = tn(grad[CHUNK:ROWS], q_ref[2 * p + j, CHUNK:ROWS])
+            gn_ref[:, at(2 * p + j, 128)] = grad
+            late = tn(grad[CHUNK:ROWS], qk_ref[CHUNK:ROWS, at(2 * p + j, 128)])
             late_ref[2 * p + j] = late
-            both = late + tn(grad[0:CHUNK], q_ref[2 * p + j, 0:CHUNK])
+            both = late + tn(grad[0:CHUNK], qk_ref[0:CHUNK, at(2 * p + j, 128)])
             after_state[p, 64 * j : 64 * j + 64] = both[0:64]
             after_state[p, 128 + j : 129 + j] = both[64:65] + both[65:66]
         after_state[p, 130:136] = jnp.zeros((6, 128), F32)
@@ -748,8 +846,7 @@
     return jnp.concatenate([body, jnp.where(first, row, 0.0)], axis=0)
 
 
-def attend_back(p, q_ref, k_ref, v_ref, gn_ref, early_ref, late_ref, before, after, trig_ref, valid_ref,
-                gate_q, gate_k, grad_ref):
+def attend_back(p, qk_ref, v_ref, gn_ref, early_ref, late_ref, before, after, trigs, gates, grad_ref):
     causal, flipped = causal_masks()
     left = left_lanes(CHUNK)
     for c in range(2):
@@ -757,7 +854,8 @@
         query, keys, value = [], [], []
         for j in range(2):
             h = 2 * p + j
-            q, k, v, g = q_ref[h, rows], k_ref[h, rows], v_ref[h, rows], gn_ref[h, rows]
+            head = at(h, 128)
+            q, k, v, g = qk_ref[rows, head], qk_ref[rows, at(HEADS + h, 128)], v_ref[rows, head], gn_ref[rows, head]
             past = prefix_state(before, p, j)
             if c == 1:
                 past = past + early_ref[h]
@@ -772,23 +870,21 @@
             gk = nn(weight, q) + nn(doubled(v), jnp.concatenate([next_high, next_low], axis=0))
             weight = jnp.where(flipped, nt(k, q), 0.0).astype(BF16)
             gv = nn(weight, g) + nt(doubled(k), jnp.concatenate([next_high, next_low], axis=1))
-            gq = gq * trig_ref[rows]
-            gk = gk * valid_ref[rows]
+            gq = gq * trigs[0, rows]
+            gk = gk * trigs[1, rows]
             query.append(gq + swap_halves(gq))
             keys.append(gk + swap_halves(gk))
             value.append(gv)
         cols = at(p, 128)
-        grad_ref[0, rows, cols] = (jnp.where(left, query[0], query[1]) * gate_q[rows, cols].astype(F32)).astype(BF16)
-        grad_ref[1, rows, cols] = (jnp.where(left, keys[0], keys[1]) * gate_k[rows, cols].astype(F32)).astype(BF16)
+        grad_ref[0, rows, cols] = (jnp.where(left, query[0], query[1]) * gates[0, rows, cols].astype(F32)).astype(BF16)
+        grad_ref[1, rows, cols] = (jnp.where(left, keys[0], keys[1]) * gates[1, rows, cols].astype(F32)).astype(BF16)
         grad_ref[2, rows, cols] = jnp.where(left, value[0], swap_halves(value[1])).astype(BF16)
 
 
-def last_kernel(x_ref, q_ref, k_ref, v_ref, gn_ref, early_ref, late_ref, before, after, trig_ref, valid_ref,
-                gate_q, gate_k, gone_ref, wq, wk, wv,
+def last_kernel(x_ref, qk_ref, v_ref, gn_ref, early_ref, late_ref, before, after, trigs, gates, gone_ref, wq, wk, wv,
                 tokens_ref, gw_q, gw_k, gw_v, vec_ref, grad_ref):
     def per_pair(p, carry):
-        attend_back(p, q_ref, k_ref, v_ref, gn_ref, early_ref, late_ref, before, after, trig_ref, valid_ref,
-                    gate_q, gate_k, grad_ref)
+        attend_back(p, qk_ref, v_ref, gn_ref, early_ref, late_ref, before, after, trigs, gates, grad_ref)
         return carry
 
     lax.fori_loop(0, PAIRS, per_pair, 0)
@@ -838,36 +934,42 @@
     vmem = pl.BlockSpec(memory_space=VMEM)
     smem = pl.BlockSpec(memory_space=pltpu.SMEM)
     anywhere = pl.BlockSpec(memory_space=pl.ANY)
-    by_head = ((HEADS, ROWS, 128), BF16)
     wide16, wide32 = ((ROWS, WIDTH), BF16), ((ROWS, WIDTH), F32)
-    table = ((ROWS, 128), F32)
+    long16, heads16 = ((ROWS, HIDDEN), BF16), ((ROWS, 128 * HEADS), BF16)
     per_head = ((HEADS, 128, 128), F32)
     packed = ((PAIRS, 136, 128), F32)
-    q, k, v, gate_q, gate_k, trig, valid, state, early = plain_call(
-        project_kernel,
-        [by_head, by_head, by_head, wide16, wide16, table, table, packed, per_head],
-        [(seq * ROWS).reshape(1), lengths, x, w_query, row(b_query), w_key, row(b_key), w_value, row(b_value)],
-        [smem, smem] + [vmem] * 7)
-    before = exchange(state, False)
-    block, gone, gn, ratio, after_state, late, gw_down, gw_up, gw_out, vec = plain_call(
+    vector = ((16, WIDTH), F32)
+    square = ((WIDTH, WIDTH), BF16)
+    kept = [long16, heads16, ((2, ROWS, WIDTH), BF16), ((2, ROWS, 128), F32), per_head, packed, wide32, wide32, wide16,
+            wide32, ((ROWS, 128), F32), wide16, long16, long16, wide32, wide16, wide16, vector]
+    (qk, v, gates, trigs, early, before, ratio, inverse, mixed, normal, scale, normed, act, slope, back, gffn, block,
+     vec) = pl.pallas_call(
+        front_kernel,
+        out_shape=[jax.ShapeDtypeStruct(*shape) for shape in kept],
+        in_specs=[smem] + [vmem] * 10 + [anywhere] * 8,
+        out_specs=[anywhere] * len(kept),
+        scratch_shapes=[VMEM(*shape) for shape in (
+            wide16, square, square, square, square, ((WIDTH, HIDDEN), BF16), ((HIDDEN, WIDTH), BF16), wide16,
+            *kept, packed, ((HEADS, ROWS, 128), F32))]
+        + [pltpu.SemaphoreType.DMA((8,)), pltpu.SemaphoreType.DMA((len(kept),))] + EXCHANGE_SCRATCH,
+        compiler_params=pltpu.CompilerParams(collective_id=2, has_side_effects=True, vmem_limit_bytes=LIMIT),
+    )(lengths, row(b_query), row(b_key), row(b_value), row(b_out), row(gain_one), row(shift_one), row(b_up),
+      row(b_down), row(gain_two), row(shift_two), x, w_query, w_key, w_value, w_out, w_up, w_down, cot)
+    gone, gn, after_state, late, gw_down, gw_up, gw_out, vec_one = plain_call(
         middle_kernel,
-        [wide16, wide32, by_head, wide32, packed, per_head,
-         ((HIDDEN, WIDTH), F32), ((WIDTH, HIDDEN), F32), ((WIDTH, WIDTH), F32), ((16, WIDTH), F32)],
-        [x, cot, q, k, v, early, before, w_out, row(b_out), row(gain_one), row(shift_one),
-         w_up, row(b_up), w_down, row(b_down), row(gain_two), row(shift_two)],
-        scratch=[
-            VMEM(*wide32), VMEM(*wide16), VMEM(*wide32), VMEM(*table), VMEM(*wide16), VMEM(*wide32),
-            VMEM((ROWS, HIDDEN), BF16), VMEM((ROWS, HIDDEN), BF16), VMEM(*wide16), VMEM(*wide16),
+        [wide32, heads16, packed, per_head, ((HIDDEN, WIDTH), F32), ((WIDTH, HIDDEN), F32), ((WIDTH, WIDTH), F32), vector],
+        [qk, ratio, inverse, mixed, normal, scale, normed, act, slope, back, gffn, w_out, w_up, row(gain_one), w_down],
+        scratch=[VMEM(*wide16), VMEM(*wide32),
             VMEM((2, TILE, WIDTH), F32), VMEM((2, WIDTH, TILE), F32), pltpu.SemaphoreType.DMA((2, 2))],
-        out_specs=[vmem] * 6 + [anywhere, anywhere, vmem, vmem])
+        out_specs=[vmem] * 4 + [anywhere, anywhere, vmem, vmem])
     after = exchange(after_state, True)
     tokens_grad, gw_q, gw_k, gw_v, vec_two = plain_call(
         last_kernel,
-        [wide32] + [((WIDTH, WIDTH), F32)] * 3 + [((16, WIDTH), F32)],
-        [x, q, k, v, gn, early, late, before, after, trig, valid, gate_q, gate_k, gone, w_query, w_key, w_value],
+        [wide32] + [((WIDTH, WIDTH), F32)] * 3 + [vector],
+        [x, qk, v, gn, early, late, before, after, trigs, gates, gone, w_query, w_key, w_value],
         scratch=[VMEM((3, ROWS, WIDTH), BF16)])
     sum_down, sum_up, sum_out, sum_query, sum_key, sum_value, sums = reduce_grads(
-        gw_down, gw_up, gw_out, gw_q, gw_k, gw_v, vec + vec_two)
+        gw_down, gw_up, gw_out, gw_q, gw_k, gw_v, vec + vec_one + vec_two)
     small = lax.dynamic_slice(sums, (0, 24 * seq), (9, 24))
     wide = lax.dynamic_slice(sums[9:15, :TILE].reshape(-1), (96 * seq,), (96,))
     return (

time: 246 us -> 241 us (0.980)
  Pallas kernels: 222 us -> 218 us
    pallas_call x0 -> x1, Pallas kernels: none -> 49.6 us  [on_device(): pl.pallas_call(front_kernel, out_shape=[jax.ShapeDtypeStruct(*shape) for...]
    pallas_call x3 -> x2, Pallas kernels: 88.2 us -> 58.3 us  [plain_call(): pl.pallas_call(kernel, out_shape=[jax.ShapeDtypeStruct(shape, dtype) for...]
    pallas_call x2 -> x1, Pallas kernels: 44.6 us -> 20.5 us  [exchange(): pl.pallas_call(kernel, out_shape=jax.ShapeDtypeStruct((PAIRS, 136, 128),...]
    unnamed x20 -> x25, local copies, waits for them, and re-layouts: 9.51 us -> 4.88 us
    reshape x9, local copies, waits for them, and re-layouts: 7.3 us -> 11.4 us  [row(): return v.reshape(1, -1)]
where the time goes in v1:
time: 241 us; the launch traced here: 240 us
  Pallas kernels  218 us (90%)
  local copies, waits for them, and re-layouts  19.3 us (8%)
    pallas_call x1, Pallas kernels, reduce_grads(): pl.pallas_call(reduce_kernel, out_shape=[jax.ShapeDtypeStruct(s, f32) for...  89.6 us
    pallas_call x2, Pallas kernels, plain_call(): pl.pallas_call(kernel, out_shape=[jax.ShapeDtypeStruct(shape, dtype) for...  58.3 us
    pallas_call x1, Pallas kernels, on_device(): pl.pallas_call(front_kernel, out_shape=[jax.ShapeDtypeStruct(*shape) for...  49.6 us
    pallas_call x1, Pallas kernels, exchange(): pl.pallas_call(kernel, out_shape=jax.ShapeDtypeStruct((PAIRS, 136, 128),...  20.5 us
    reshape x9, local copies, waits for them, and re-layouts, row(): return v.reshape(1, -1)  11.4 us
    unnamed x25, local copies, waits for them, and re-layouts  4.88 us

profile of v1, /device:TPU:0, one launch (start us, length us, event | category | flops | bytes accessed | tf_op | source)
XLA Modules:
  0.0 240.1 jit_solution(7295701536910258730)
XLA Ops:
  0.7 1.3 reshape.92.gain1
  1.9 1.3 reshape.88.bq
  3.2 1.3 reshape.89.bk
  4.5 1.3 reshape.90.bv
  5.7 1.3 reshape.91.bo
  7.0 1.3 reshape.93.shift1
  8.3 1.3 reshape.95.bdown
  9.5 1.3 reshape.96.gain2
  10.8 1.3 reshape.97.shift2
  12.7 49.6 %shard_map.322 = (bf16[512,3072]{1,0:T(8,128)(2,1)}, bf16[512,1536]{1,0:T(8,128)(2,1)}, bf16[2,512,768]{2,1,0:T(8,128)(2,1)}, f32[2,512,128]{2,1,0:T(8,128)}, f3...) custom-call(s32[1]{0:T(128)S(6)} %copy.44.len_ref, ...), custom_call_target="tpu_custom_call" | custom-call | tf_op jit(solution)/shard_map/pallas_call | solution.py:946
  62.3 30.1 %shard_map.323 = (f32[512,768]{1,0:T(8,128)}, bf16[512,1536]{1,0:T(8,128)(2,1)}, f32[6,136,128]{2,1,0:T(8,128)}, f32[12,128,128]{2,1,0:T(8,128)}, f32[3072,768]{...) custom-call(bf16[512,3072]{1,0:T(8,128)(2,1)} %get-tuple-element.57.qk_ref, ...), custom_call_target="tpu_custom_call" | custom-call | tf_op jit(solution)/shard_map/pallas_call | solution.py:915
  92.4 20.5 %shard_map.324.after = f32[6,136,128]{2,1,0:T(8,128)} custom-call(f32[6,136,128]{2,1,0:T(8,128)} %get-tuple-element.73.refs_0_), custom_call_target="tpu_custom_call" | custom-call | tf_op jit(solution)/shard_map/pallas_call | solution.py:269
  112.9 0.0 copy-start.7
  112.9 0.0 copy-start.8
  112.9 28.2 %shard_map.325 = (f32[512,768]{1,0:T(8,128)}, f32[768,768]{1,0:T(8,128)}, f32[768,768]{1,0:T(8,128)}, f32[768,768]{1,0:T(8,128)}, f32[16,768]{1,0:T(8,128)}) custom-call(bf16[512,768]{1,0:T(8,128)(2,1)} %bitcast.32, bf16[512,3072]{1,0:T(8,128)(2,1)} %get-tuple-element.57.qk_ref, bf16[512,1536]{1,0:T(8,128)(2,1)} %get-tuple-element.58.v_ref, ...), custom_call_target="tpu_custom_call" | custom-call | tf_op jit(solution)/shard_map/pallas_call | solution.py:915
  141.1 0.0 copy-done.7
  141.1 0.0 copy-done.8
  141.2 1.4 add_add_fusion.vec
  142.6 0.0 copy-start
  142.6 89.6 %shard_map.326 = (f32[96,768]{1,0:T(8,128)}, f32[24,3072]{1,0:T(8,128)}, f32[24,768]{1,0:T(8,128)}, f32[24,768]{1,0:T(8,128)}, f32[24,768]{1,0:T(8,128)}, /*index=5*/f32[24,768]{1,0:T(8,128)}, f32[16,768]{1,0:T(8,128)}) custom-call(f32[4,4,2,4,24,768]{5,4,3,2,1,0:T(8,128)} %bitcast.29, f32[4,4,2,24,3072]{4,3,2,1,0:T(8,128)} %bitcast.30, ...), custom_call_target="tpu_custom_call" | custom-call | tf_op jit(solution)/shard_map/pallas_call | solution.py:810
  232.2 0.0 copy-start.6
  232.2 0.0 copy-start.5
  232.2 0.0 copy-start.4
  232.2 0.0 copy-start.3
  232.2 0.0 copy-start.2
  232.3 0.0 copy-start.1
  232.3 0.8 slice.36
  233.1 0.6 dynamic_slice.7
  233.7 1.6 dynamic-slice_bitcast_fusion
  235.3 0.0 copy-done
  235.3 0.9 copy.45
  236.2 0.0 copy-done.6
  236.2 0.6 copy.46
  236.8 0.0 copy-done.5
  236.8 0.6 copy.47
  237.4 0.0 copy-done.4
  237.4 0.6 copy.48
  238.1 0.0 copy-done.3
  238.1 0.6 copy.49
  238.7 0.0 copy-done.2
  238.7 0.7 copy.50
  239.4 0.0 copy-done.1
  239.4 0.7 copy.51
  (1 shorter events, 0.0 us)
Async XLA Ops:
  112.9 28.2 %copy-start.7 = (f32[16,768]{1,0:T(8,128)S(1)}, f32[16,768]{1,0:T(8,128)}, u32[]{:S(2)}) copy-start(f32[16,768]{1,0:T(8,128)} %get-tuple-element.84) | copy-start | bytes 147460
  112.9 28.2 %copy-start.8 = (f32[16,768]{1,0:T(8,128)S(1)}, f32[16,768]{1,0:T(8,128)}, u32[]{:S(2)}) copy-start(f32[16,768]{1,0:T(8,128)} %get-tuple-element.85) | copy-start | bytes 147460
  142.6 92.7 %copy-start = (bf16[512,768]{1,0:T(8,128)(2,1)S(1)}, bf16[512,768]{1,0:T(8,128)(2,1)}, u32[]{:S(2)}) copy-start(bf16[512,768]{1,0:T(8,128)(2,1)} %get-tuple-element.56) | copy-start | bytes 2359300
  232.2 4.0 %copy-start.6 = (f32[24,768]{1,0:T(8,128)S(1)}, f32[24,768]{1,0:T(8,128)}, u32[]{:S(2)}) copy-start(f32[24,768]{1,0:T(8,128)} %get-tuple-element.123) | copy-start | bytes 221188
  232.2 4.6 %copy-start.5 = (f32[24,768]{1,0:T(8,128)S(1)}, f32[24,768]{1,0:T(8,128)}, u32[]{:S(2)}) copy-start(f32[24,768]{1,0:T(8,128)} %get-tuple-element.125) | copy-start | bytes 221188
  232.2 5.2 %copy-start.4 = (f32[24,768]{1,0:T(8,128)S(1)}, f32[24,768]{1,0:T(8,128)}, u32[]{:S(2)}) copy-start(f32[24,768]{1,0:T(8,128)} %get-tuple-element.127) | copy-start | bytes 221188
  232.2 5.8 %copy-start.3 = (f32[24,768]{1,0:T(8,128)S(1)}, f32[24,768]{1,0:T(8,128)}, u32[]{:S(2)}) copy-start(f32[24,768]{1,0:T(8,128)} %get-tuple-element.129) | copy-start | bytes 221188
  232.2 6.5 %copy-start.2 = (f32[24,3072]{1,0:T(8,128)S(1)}, f32[24,3072]{1,0:T(8,128)}, u32[]{:S(2)}) copy-start(f32[24,3072]{1,0:T(8,128)} %get-tuple-element.133) | copy-start | bytes 884740
  232.3 7.2 %copy-start.1 = (f32[96,768]{1,0:T(8,128)S(1)}, f32[96,768]{1,0:T(8,128)}, u32[]{:S(2)}) copy-start(f32[96,768]{1,0:T(8,128)} %get-tuple-element.135) | copy-start | bytes 884740

commit v2 on v1

--- a/solution.py
+++ b/solution.py
@@ -25,6 +25,7 @@
 TILE = 512
 VMEM = pltpu.VMEM
 LIMIT = 60 * 2**20
+BACK_LIMIT = 63 * 2**20
 
 
 def nn(a, b):
@@ -254,29 +255,6 @@
     pl.semaphore_wait(pltpu.get_barrier_semaphore(), 1 + 3 * len(axes))
 
 
-def exchange_kernel(reverse, pay, out, *scratch):
-    greet(("seq_0", "seq_1"))
-    greeted(("seq_0", "seq_1"))
-    first, second, third, fourth, fifth = exchange_steps(pay, out, *scratch, reverse)
-    fifth(fourth(third(second(first()))))
-
-
-def exchange(pay, reverse):
-    def kernel(*refs):
-        exchange_kernel(reverse, *refs)
-
-    vmem = pl.BlockSpec(memory_space=VMEM)
-    return pl.pallas_call(
-        kernel,
-        out_shape=jax.ShapeDtypeStruct((PAIRS, 136, 128), F32),
-        in_specs=[vmem],
-        out_specs=vmem,
-        scratch_shapes=EXCHANGE_SCRATCH,
-        compiler_params=pltpu.CompilerParams(
-            collective_id=1 if reverse else 2, has_side_effects=True, vmem_limit_bytes=LIMIT),
-    )(pay)
-
-
 def causal_masks():
     row = lax.broadcasted_iota(jnp.int32, (CHUNK, CHUNK), 0)
     col = lax.broadcasted_iota(jnp.int32, (CHUNK, CHUNK), 1)
@@ -486,90 +464,6 @@
         copy.wait()
 
 
-def middle_kernel(qk_ref, ratio_ref, inverse_ref, mixed_ref, normal_ref, scale_ref, normed_ref, act_ref, slope_ref,
-                  acc_ref, gffn_ref, wo, wup, gain1, wdown,
-                  gone_ref, gn_ref, after_state, late_ref, gw_down, gw_up, gw_out, vec_ref,
-                  gproj_ref, scratch_ref, tile_a, tile_b, store_sem):
-    vec_ref[...] = jnp.zeros_like(vec_ref)
-
-    def note(k, value):
-        vec_ref[k : k + 1, :] += value
-
-    gone_ref[...] = acc_ref[...]
-
-    def stores(t, slot):
-        cols = at(t, TILE)
-        return (pltpu.make_async_copy(tile_a.at[slot], gw_down.at[cols], store_sem.at[0, slot]),
-                pltpu.make_async_copy(tile_b.at[slot], gw_up.at[:, cols], store_sem.at[1, slot]))
-
-    def feed_back(t, carry):
-        cols = at(t, TILE)
-        slot = lax.rem(t, 2)
-
-        @pl.when(t >= 2)
-        def _():
-            for copy in stores(t - 2, slot):
-                copy.wait()
-
-        gffn = gffn_ref[...]
-        gpre = (nt(gffn, wdown[cols]) * slope_ref[:, cols].astype(F32)).astype(BF16)
-        total = column(gpre.astype(F32))
-        vec_ref[pl.ds(9 + t, 1), 0:TILE] = total
-        tile_a[slot] = tn(act_ref[:, cols], gffn)
-        tile_b[slot] = tn(normed_ref[...], gpre)
-        gone_ref[...] += nt(gpre, wup[:, cols])
-        for copy in stores(t, slot):
-            copy.start()
-        return carry
-
-    tiles = HIDDEN // TILE
-    lax.fori_loop(0, tiles, feed_back, 0)
-
-    def first_back(r, carry):
-        rows = at(r, 128)
-        normal = normal_ref[rows]
-        scale = scale_ref[rows, 0:1]
-        grad = gone_ref[rows]
-        note(4, column(grad * normal))
-        note(5, column(grad))
-        back = norm_back(grad, normal, scale, gain1[...])
-        gone_ref[rows] = back
-        low = back.astype(BF16)
-        gproj_ref[rows] = low
-        note(3, column(low.astype(F32)))
-        scratch_ref[rows] = nt(low, wo[...])
-        return carry
-
-    lax.fori_loop(0, ROWS // 128, first_back, 0)
-    gw_out[...] = tn(mixed_ref[...], gproj_ref[...])
-
-    def heads_back(p, carry):
-        cols = at(p, 128)
-        lane = lax.broadcasted_iota(jnp.int32, (ROWS, 128), 1)
-        left = lane < 64
-        gnum = (scratch_ref[:, cols] * inverse_ref[:, cols]).astype(BF16).astype(F32)
-        product = gnum * ratio_ref[:, cols]
-        for j in range(2):
-            mine = jnp.where(left, product, 0.0) if j == 0 else jnp.where(left, 0.0, product)
-            gden = jnp.broadcast_to(-jnp.sum(mine, axis=1, keepdims=True), (ROWS, 128))
-            high = gden.astype(BF16).astype(F32)
-            ends = jnp.where(lane == 64, high, jnp.where(lane == 65, gden - high, 0.0))
-            grad = jnp.where(left, gnum if j == 0 else swap_halves(gnum), ends).astype(BF16)
-            gn_ref[:, at(2 * p + j, 128)] = grad
-            late = tn(grad[CHUNK:ROWS], qk_ref[CHUNK:ROWS, at(2 * p + j, 128)])
-            late_ref[2 * p + j] = late
-            both = late + tn(grad[0:CHUNK], qk_ref[0:CHUNK, at(2 * p + j, 128)])
-            after_state[p, 64 * j : 64 * j + 64] = both[0:64]
-            after_state[p, 128 + j : 129 + j] = both[64:65] + both[65:66]
-        after_state[p, 130:136] = jnp.zeros((6, 128), F32)
-        return carry
-
-    lax.fori_loop(0, PAIRS, heads_back, 0)
-    for t in (tiles - 2, tiles - 1):
-        for copy in stores(t, t % 2):
-            copy.wait()
-
-
 ORDERS = ((1, 0, 2), (0, 2, 1), (2, 1, 0))
 SUBS = 9
 COLS = 256
@@ -595,248 +489,177 @@
         total *= n
 
     def step(k, carry):
-        at, rest = [], k
+        where, rest = [], k
         for n in reversed(lead):
-            at.append(lax.rem(rest, n))
+            where.append(lax.rem(rest, n))
             rest = rest // n
-        at = tuple(reversed(at))
-        value = dst[at]
+        where = tuple(reversed(where))
+        value = dst[where]
         for src in srcs:
-            value = value + src[at]
-        dst[at] = value
+            value = value + src[where]
+        dst[where] = value
         return carry
 
     lax.fori_loop(0, total, step, 0)
 
 
-def reduce_kernel(
-    down, up, w_o, w_q, w_k, w_v, vec,
-    out_down, out_up, out_o, out_q, out_k, out_v, out_vec,
-    own, core_in, first, second, third, done, vecs,
-    load_sem, core_send, core_recv, send, recv, vsend, vrecv,
-):
+GROUPS = ((0, 0, 256), (1, 0, 256), (0, 0, 128), (0, 128, 128))
+DONE = (0, 1, 2, 2)
+
+
+class Reduction:
+    def __init__(self, stage, sums, first, second, third, done, core_send, core_recv, send, recv):
+        self.stage, self.sums, self.first, self.second, self.third, self.done = stage, sums, first, second, third, done
+        self.core_send, self.core_recv, self.send, self.recv = core_send, core_recv, send, recv
+        self.me = tuple(lax.axis_index(a) for a in AX)
+        self.core = lax.axis_index(CORE)
+        self.other = 1 - self.core
+        self.moves, self.flight = {0: [], 1: [], 2: [], 3: []}, {}
+
+    def swap(self, g, s, part):
+        slot, start, width = GROUPS[g]
+        where = (part,) if g == 0 else (slice(None), slice(None), part, slice(None), pl.ds(start, width))
+        return pltpu.make_async_remote_copy(
+            src_ref=self.stage.at[(s, self.other, *where)], dst_ref=self.sums.at[(slot, s, *where)],
+            send_sem=self.core_send.at[g, s, part], recv_sem=self.core_recv.at[g, s, part],
+            device_id={CORE: self.other}, device_id_type=MESH)
+
+    def remote(self, src, dst, g, s, k, axis, d):
+        copy = pltpu.make_async_remote_copy(
+            src_ref=src, dst_ref=dst, send_sem=self.send.at[g, s, k], recv_sem=self.recv.at[g, s, k],
+            device_id={AX[axis]: rot(self.me[axis], d)}, device_id_type=MESH)
+        copy.start()
+        self.moves[g].append(copy)
+        return copy
+
+    def views(self, g, s):
+        slot, start, width = GROUPS[g]
+        cols = pl.ds(start, width)
+        return (self.sums.at[slot, s, :, :, :, :, cols], self.first.at[slot, s, :, :, :, :, cols],
+                self.second.at[slot, s, :, :, :, cols], self.third.at[slot, s, :, :, cols],
+                self.done.at[DONE[g], s, :, :, cols], self.stage.at[s, self.core, :, :, :, :, cols])
+
+    def begin(self, g, s):
+        mine, inbox, _, _, _, own = self.views(g, s)
+        for part in range(4):
+            copy = self.swap(g, s, part)
+            copy.wait_recv()
+            copy.wait_send()
+        add_blocks(mine, [own], (4, 4))
+        order = ORDERS[s]
+        ax = order[0]
+        i = self.me[ax]
+        lo, hi = pl.ds(0, 2), pl.ds(2, 2)
+        far = rot(i, 2)
+        self.flight[g, s, 0] = (
+            self.remote(halved(mine, order, far, lo), inbox.at[0, lo], g, s, 0, ax, 1),
+            self.remote(halved(mine, order, far, hi), inbox.at[0, hi], g, s, 1, ax, 3),
+        )
+        self.flight[g, s, 1] = (
+            self.remote(halved(mine, order, rot(i, 1), hi), inbox.at[1, hi], g, s, 2, ax, 1),
+            self.remote(halved(mine, order, rot(i, 3), lo), inbox.at[2, lo], g, s, 3, ax, 3),
+        )
+
+    def relay(self, g, s):
+        mine, inbox = self.views(g, s)[:2]
+        order = ORDERS[s]
+        ax = order[0]
+        i = self.me[ax]
+        lo, hi = pl.ds(0, 2), pl.ds(2, 2)
+        first, second = self.flight[g, s, 0]
+        first.wait_recv()
+        part = halved(mine, order, rot(i, 1), lo)
+        add_blocks(part, [inbox.at[0, lo]], (2, 4))
+        third = self.remote(part, inbox.at[1, lo], g, s, 4, ax, 1)
+        second.wait_recv()
+        part = halved(mine, order, rot(i, 3), hi)
+        add_blocks(part, [inbox.at[0, hi]], (2, 4))
+        fourth = self.remote(part, inbox.at[2, hi], g, s, 5, ax, 3)
+        self.flight[g, s, 1] += (third, fourth)
+
+    def middle(self, g, s):
+        mine, inbox, second = self.views(g, s)[:3]
+        order = ORDERS[s]
+        for copy in self.flight[g, s, 1]:
+            copy.wait_recv()
+        i, ax = self.me[order[0]], order[1]
+        add_blocks(cell(mine, order, (i,)), [inbox.at[1], inbox.at[2]], (4,))
+        self.flight[g, s, 2] = [
+            self.remote(cell(mine, order, (i, rot(self.me[ax], d))), second.at[k], g, s, 6 + k, ax, d)
+            for k, d in enumerate(DIRECT)
+        ]
+
+    def last(self, g, s):
+        mine, _, second, third = self.views(g, s)[:4]
+        order = ORDERS[s]
+        for copy in self.flight[g, s, 2]:
+            copy.wait_recv()
+        where = (self.me[order[0]], self.me[order[1]])
+        add_blocks(cell(mine, order, where), [second.at[k] for k in range(3)], (4,))
+        ax = order[2]
+        self.flight[g, s, 3] = [
+            self.remote(cell(mine, order, (*where, rot(self.me[ax], d))), third.at[k], g, s, 9 + k, ax, d)
+            for k, d in enumerate(DIRECT)
+        ]
+
+    def spread(self, g, s):
+        mine, _, _, third, done = self.views(g, s)[:5]
+        for copy in self.flight[g, s, 3]:
+            copy.wait_recv()
+        y, x, z = self.me
+        done[z] = mine[y, x, z] + third[0] + third[1] + third[2]
+        self.flight[g, s, 4] = [
+            self.remote(done.at[z], done.at[z], g, s, 12 + k, 2, d) for k, d in enumerate(DIRECT)
+        ]
+
+    def finish(self, g, s):
+        for copy in self.flight[g, s, 4]:
+            copy.wait_recv()
+
+    def sent(self, g):
+        for copy in self.moves[g]:
+            copy.wait_send()
+
+    def each(self, step, g):
+        for s in range(3):
+            step(g, s)
+
+
+def vector_steps(vec, vecs, send, recv):
     me = tuple(lax.axis_index(a) for a in AX)
     core = lax.axis_index(CORE)
-    other = 1 - core
-    barrier = pltpu.get_barrier_semaphore()
-    pl.semaphore_signal(barrier, inc=1, device_id={CORE: other}, device_id_type=MESH)
-    for axis in range(3):
-        for d in DIRECT:
-            pl.semaphore_signal(barrier, inc=1, device_id={AX[axis]: rot(me[axis], d)}, device_id_type=MESH)
-    pl.semaphore_wait(barrier, 10)
-
-    def source(s, b, half):
-        columns = pl.ds(COLS * (s % 3), COLS)
-        if s < 3:
-            return down.at[:, :, half, b, :, columns]
-        if s < 6:
-            return up.at[:, :, half, :, pl.ds(768 * b + COLS * (s % 3), COLS)]
-        return (w_o, w_q, w_k, w_v)[b].at[:, :, half, :, columns]
-
-    loads, swaps, moves = {}, {}, []
-    for s in (0, 4, 8, 3, 7, 2, 6, 1, 5):
-        for b in range(4):
-            swap = pltpu.make_async_remote_copy(
-                src_ref=source(s, b, other), dst_ref=core_in.at[s, :, :, b],
-                send_sem=core_send.at[s, b], recv_sem=core_recv.at[s, b],
-                device_id={CORE: other}, device_id_type=MESH)
-            swap.start()
-            load = pltpu.make_async_copy(source(s, b, core), own.at[s, :, :, b], load_sem.at[s, b])
-            load.start()
-            loads[s, b], swaps[s, b] = load, swap
-
-    def remote(src, dst, s, k, axis, d):
-        copy = pltpu.make_async_remote_copy(
-            src_ref=src, dst_ref=dst, send_sem=send.at[s, k], recv_sem=recv.at[s, k],
-            device_id={AX[axis]: rot(me[axis], d)}, device_id_type=MESH)
-        copy.start()
-        moves.append(copy)
-        return copy
-
-    flight = {}
-
-    def begin(s):
-        order = ORDERS[s % 3]
-        i = me[order[0]]
-        mine, inbox = own.at[s], first.at[s]
-        for b in range(4):
-            loads[s, b].wait()
-            swaps[s, b].wait_recv()
-        add_blocks(mine, [core_in.at[s]], (4, 4, 4))
-        lo, hi = pl.ds(0, 2), pl.ds(2, 2)
-        far = rot(i, 2)
-        ax = order[0]
-        flight[s, "a"] = (
-            remote(halved(mine, order, far, lo), inbox.at[0, pl.ds(0, 2)], s, 0, ax, 1),
-            remote(halved(mine, order, far, hi), inbox.at[0, pl.ds(2, 2)], s, 1, ax, 3),
-        )
-        flight[s, "b"] = (
-            remote(halved(mine, order, rot(i, 1), hi), inbox.at[1, pl.ds(2, 2)], s, 2, ax, 1),
-            remote(halved(mine, order, rot(i, 3), lo), inbox.at[2, pl.ds(0, 2)], s, 3, ax, 3),
-        )
-
-    def relay(s):
-        order = ORDERS[s % 3]
-        i = me[order[0]]
-        mine, inbox = own.at[s], first.at[s]
-        lo, hi = pl.ds(0, 2), pl.ds(2, 2)
-        ax = order[0]
-        flight[s, "a"][0].wait_recv()
-        part = halved(mine, order, rot(i, 1), lo)
-        add_blocks(part, [inbox.at[0, pl.ds(0, 2)]], (2, 4))
-        c0 = remote(part, inbox.at[1, pl.ds(0, 2)], s, 4, ax, 1)
-        flight[s, "a"][1].wait_recv()
-        part = halved(mine, order, rot(i, 3), hi)
-        add_blocks(part, [inbox.at[0, pl.ds(2, 2)]], (2, 4))
-        c1 = remote(part, inbox.at[2, pl.ds(2, 2)], s, 5, ax, 3)
-        flight[s, "b"] += (c0, c1)
-
-    def middle(s):
-        order = ORDERS[s % 3]
-        mine = own.at[s]
-        for copy in flight[s, "b"]:
-            copy.wait_recv()
-        i = me[order[0]]
-        add_blocks(cell(mine, order, (i,)), [first.at[s, 1], first.at[s, 2]], (4, 4))
-        ax = order[1]
-        flight[s, 2] = [
-            remote(cell(mine, order, (i, rot(me[ax], d))), second.at[s, k], s, 6 + k, ax, d)
-            for k, d in enumerate(DIRECT)
-        ]
-
-    def last(s):
-        order = ORDERS[s % 3]
-        mine = own.at[s]
-        for copy in flight[s, 2]:
-            copy.wait_recv()
-        at = (me[order[0]], me[order[1]])
-        add_blocks(cell(mine, order, at), [second.at[s, k] for k in range(3)], (4,))
-        ax = order[2]
-        flight[s, 3] = [
-            remote(cell(mine, order, (*at, rot(me[ax], d))), third.at[s, k], s, 9 + k, ax, d)
-            for k, d in enumerate(DIRECT)
-        ]
-
-    def spread(s):
-        for copy in flight[s, 3]:
-            copy.wait_recv()
-        done[s, me[2]] = own[s, me[0], me[1], me[2]] + third[s, 0] + third[s, 1] + third[s, 2]
-        flight[s, 4] = [
-            remote(done.at[s, me[2]], done.at[s, me[2]], s, 12 + k, 2, d)
-            for k, d in enumerate(DIRECT)
-        ]
-
-    def finish(s):
-        for copy in flight[s, 4]:
-            copy.wait_recv()
-        c = pl.ds(COLS * (s % 3), COLS)
-        for b in range(4):
-            if s < 3:
-                out_down[24 * b : 24 * b + 24, c] = done[s, b]
-            elif s < 6:
-                out_up[:, pl.ds(768 * b + COLS * (s % 3), COLS)] = done[s, b]
-            else:
-                (out_o, out_q, out_k, out_v)[b][:, c] = done[s, b]
-
-    vecs[0] = vec[...]
-    vmoves = {}
-
-    def vector_send(stage):
+    moves = {}
+    bases = (0, 1, 4, 7)
+
+    def start(stage):
         if stage == 0:
-            targets = [{CORE: other}]
+            targets = [{CORE: 1 - core}]
+            vecs[0] = vec[...]
         else:
             ax = stage - 1
             targets = [{AX[ax]: rot(me[ax], d)} for d in DIRECT]
-        base = (0, 1, 4, 7)[stage]
-        vmoves[stage] = []
+        moves[stage] = []
         for k, target in enumerate(targets):
+            n = bases[stage] + k
             copy = pltpu.make_async_remote_copy(
-                src_ref=vecs.at[stage], dst_ref=vecs.at[5 + base + k],
-                send_sem=vsend.at[base + k], recv_sem=vrecv.at[base + k],
+                src_ref=vecs.at[stage], dst_ref=vecs.at[5 + n], send_sem=send.at[n], recv_sem=recv.at[n],
                 device_id=target, device_id_type=MESH)
             copy.start()
-            vmoves[stage].append(copy)
-
-    def vector_sum(stage):
-        base = (0, 1, 4, 7)[stage]
+            moves[stage].append(copy)
+
+    def end(stage):
         total = vecs[stage]
-        for k, copy in enumerate(vmoves[stage]):
+        for k, copy in enumerate(moves[stage]):
             copy.wait_recv()
-            total = total + vecs[5 + base + k]
+            total = total + vecs[5 + bases[stage] + k]
         vecs[stage + 1] = total
 
-    G = [(0, 4, 8), (3, 7, 2), (6, 1, 5)]
-
-    def run(step, g):
-        for s in G[g]:
-            step(s)
-
-    vector_send(0)
-    run(begin, 0)
-    vector_sum(0)
-    vector_send(1)
-    run(relay, 0)
-    run(begin, 1)
-    run(middle, 0)
-    vector_sum(1)
-    vector_send(2)
-    run(relay, 1)
-    run(begin, 2)
-    run(last, 0)
-    run(middle, 1)
-    run(relay, 2)
-    run(spread, 0)
-    vector_sum(2)
-    vector_send(3)
-    run(last, 1)
-    run(middle, 2)
-    run(finish, 0)
-    run(spread, 1)
-    run(last, 2)
-    vector_sum(3)
-    out_vec[...] = vecs[4]
-    run(finish, 1)
-    run(spread, 2)
-    run(finish, 2)
-    for copy in [*moves, *swaps.values(), *(c for cs in vmoves.values() for c in cs)]:
-        copy.wait_send()
-
-
-def reduce_grads(down, up, w_o, w_q, w_k, w_v, vec):
-    f32 = jnp.float32
-    shapes = [(96, 768), (24, 3072), (24, 768), (24, 768), (24, 768), (24, 768), (16, 768)]
-    any_spec = pl.BlockSpec(memory_space=pl.ANY)
-    vmem = pl.BlockSpec(memory_space=pltpu.VMEM)
-    return pl.pallas_call(
-        reduce_kernel,
-        out_shape=[jax.ShapeDtypeStruct(s, f32) for s in shapes],
-        in_specs=[any_spec] * 6 + [vmem],
-        out_specs=[vmem] * 7,
-        scratch_shapes=[
-            pltpu.VMEM((SUBS, 4, 4, 4, 24, COLS), f32),
-            pltpu.VMEM((SUBS, 4, 4, 4, 24, COLS), f32),
-            pltpu.VMEM((SUBS, 3, 4, 4, 24, COLS), f32),
-            pltpu.VMEM((SUBS, 3, 4, 24, COLS), f32),
-            pltpu.VMEM((SUBS, 3, 24, COLS), f32),
-            pltpu.VMEM((SUBS, 4, 24, COLS), f32),
-            pltpu.VMEM((15, 16, 768), f32),
-            pltpu.SemaphoreType.DMA((SUBS, 4)),
-            pltpu.SemaphoreType.DMA((SUBS, 4)),
-            pltpu.SemaphoreType.DMA((SUBS, 4)),
-            pltpu.SemaphoreType.DMA((SUBS, 15)),
-            pltpu.SemaphoreType.DMA((SUBS, 15)),
-            pltpu.SemaphoreType.DMA((10,)),
-            pltpu.SemaphoreType.DMA((10,)),
-        ],
-        compiler_params=pltpu.CompilerParams(
-            collective_id=0, has_side_effects=True, vmem_limit_bytes=60 * 2**20
-        ),
-    )(
-        down.reshape(4, 4, 2, 4, 24, 768),
-        up.reshape(4, 4, 2, 24, 3072),
-        *(w.reshape(4, 4, 2, 24, 768) for w in (w_o, w_q, w_k, w_v)),
-        vec,
-    )
+    def sent():
+        for copies in moves.values():
+            for copy in copies:
+                copy.wait_send()
+
+    return start, end, sent
 
 
 def suffix_state(after, p, j):
@@ -846,7 +669,7 @@
     return jnp.concatenate([body, jnp.where(first, row, 0.0)], axis=0)
 
 
-def attend_back(p, qk_ref, v_ref, gn_ref, early_ref, late_ref, before, after, trigs, gates, grad_ref):
+def attend_back_local(p, act, bufu, early_ref, before, trigs, ratio_ref, inverse_ref, grads):
     causal, flipped = causal_masks()
     left = left_lanes(CHUNK)
     for c in range(2):
@@ -854,72 +677,327 @@
         query, keys, value = [], [], []
         for j in range(2):
             h = 2 * p + j
-            head = at(h, 128)
-            q, k, v, g = qk_ref[rows, head], qk_ref[rows, at(HEADS + h, 128)], v_ref[rows, head], gn_ref[rows, head]
+            q, k = bufu[rows, at(h, 128)], bufu[rows, at(HEADS + h, 128)]
+            v, g = act[rows, at(h, 128)], act[rows, at(HEADS + h, 128)]
             past = prefix_state(before, p, j)
             if c == 1:
                 past = past + early_ref[h]
-            future = suffix_state(after, p, j)
-            if c == 0:
-                future = future + late_ref[h]
-            past_high, past_low = halves(past)
-            next_high, next_low = halves(future)
+            high, low = halves(past)
             weight = jnp.where(causal, nt(g, v), 0.0).astype(BF16)
-            gq = nn(weight, k) + nn(doubled(g), jnp.concatenate([past_high, past_low], axis=0))
+            gq = nn(weight, k) + nn(doubled(g), jnp.concatenate([high, low], axis=0))
             weight = jnp.where(flipped, nt(v, g), 0.0).astype(BF16)
-            gk = nn(weight, q) + nn(doubled(v), jnp.concatenate([next_high, next_low], axis=0))
+            gk = nn(weight, q)
             weight = jnp.where(flipped, nt(k, q), 0.0).astype(BF16)
-            gv = nn(weight, g) + nt(doubled(k), jnp.concatenate([next_high, next_low], axis=1))
+            value.append(nn(weight, g))
             gq = gq * trigs[0, rows]
             gk = gk * trigs[1, rows]
             query.append(gq + swap_halves(gq))
             keys.append(gk + swap_halves(gk))
-            value.append(gv)
         cols = at(p, 128)
-        grad_ref[0, rows, cols] = (jnp.where(left, query[0], query[1]) * gates[0, rows, cols].astype(F32)).astype(BF16)
-        grad_ref[1, rows, cols] = (jnp.where(left, keys[0], keys[1]) * gates[1, rows, cols].astype(F32)).astype(BF16)
-        grad_ref[2, rows, cols] = jnp.where(left, value[0], swap_halves(value[1])).astype(BF16)
-
-
-def last_kernel(x_ref, qk_ref, v_ref, gn_ref, early_ref, late_ref, before, after, trigs, gates, gone_ref, wq, wk, wv,
-                tokens_ref, gw_q, gw_k, gw_v, vec_ref, grad_ref):
-    def per_pair(p, carry):
-        attend_back(p, qk_ref, v_ref, gn_ref, early_ref, late_ref, before, after, trigs, gates, grad_ref)
-        return carry
-
-    lax.fori_loop(0, PAIRS, per_pair, 0)
-    vec_ref[...] = jnp.zeros_like(vec_ref)
-    for i, out in enumerate((gw_q, gw_k, gw_v)):
-        vec_ref[i : i + 1, :] = column(grad_ref[i].astype(F32))
-
-        def product(n, carry):
-            cols = at(n, 256)
-            out[:, cols] = tn(x_ref[...], grad_ref[i, :, cols])
-            return carry
-
-        lax.fori_loop(0, WIDTH // 256, product, 0)
+        gate = bufu[ROWS:WIDTH, at(PAIRS * c + p, 128)].astype(F32)
+        grads[rows, cols] = (jnp.where(left, query[0], query[1]) * gate).astype(BF16)
+        ratio_ref[rows, cols] = jnp.where(left, keys[0], keys[1])
+        inverse_ref[rows, cols] = jnp.where(left, value[0], swap_halves(value[1]))
+
+
+def attend_back_later(p, act, bufu, late_ref, after, trigs, ratio_ref, inverse_ref, grads):
+    left = left_lanes(CHUNK)
+    for c in range(2):
+        rows = slice(CHUNK * c, CHUNK * c + CHUNK)
+        keys, value = [], []
+        for j in range(2):
+            h = 2 * p + j
+            k, v = bufu[rows, at(HEADS + h, 128)], act[rows, at(h, 128)]
+            future = suffix_state(after, p, j)
+            if c == 0:
+                future = future + late_ref[h]
+            high, low = halves(future)
+            gk = nn(doubled(v), jnp.concatenate([high, low], axis=0)) * trigs[1, rows]
+            keys.append(gk + swap_halves(gk))
+            value.append(nt(doubled(k), jnp.concatenate([high, low], axis=1)))
+        cols = at(p, 128)
+        gate = bufu[ROWS:WIDTH, at(2 * PAIRS + PAIRS * c + p, 128)].astype(F32)
+        gk = (ratio_ref[rows, cols] + jnp.where(left, keys[0], keys[1])) * gate
+        grads[rows, at(PAIRS + p, 128)] = gk.astype(BF16)
+        gv = inverse_ref[rows, cols] + jnp.where(left, value[0], swap_halves(value[1]))
+        grads[rows, at(2 * PAIRS + p, 128)] = gv.astype(BF16)
+
+
+def back_kernel(gain1, qk_hbm, v_hbm, gates_hbm, trigs_hbm, early_hbm, before_hbm, ratio_hbm, inverse_hbm, mixed_hbm,
+                normal_hbm, scale_hbm, normed_hbm, act_hbm, slope_hbm, back_hbm, gffn_hbm, vec_hbm,
+                x_hbm, wq_hbm, wk_hbm, wv_hbm, wo_hbm, wup_hbm, wdown_hbm,
+                tokens_out, done_out, vec_out,
+                trigs, early_ref, before, ratio_ref, inverse_ref, mixed_ref, normal_ref, scale_ref, normed_ref,
+                act, slope, acc_ref, gffn_ref, vec_ref, wo, bufu, bufd,
+                late_ref, pay, after, turned, stage, sums, first_in, second_in, third_in, done, vecs,
+                load_sem, store_sem, core_send, core_recv, send, recv, vec_send, vec_recv, free_sem, *scratch):
+    everywhere = ("seq_0", "seq_1", "batch")
+    greet(everywhere)
+    loads = {}
+
+    def load(name, src, dst):
+        copy = pltpu.make_async_copy(src, dst, load_sem.at[len(loads)])
+        copy.start()
+        loads[name] = copy
+
+    def ready(*names):
+        for name in names:
+            loads[name].wait()
+
+    load("gffn", gffn_hbm, gffn_ref)
+    load("act", act_hbm, act)
+    load("wdown", wdown_hbm, bufd)
+    load("slope", slope_hbm, slope)
+    load("wup", wup_hbm, bufu)
+    load("back", back_hbm, acc_ref)
+    load("vec", vec_hbm, vec_ref)
+    load("normed", normed_hbm, normed_ref)
+    load("normal", normal_hbm, normal_ref)
+    load("scale", scale_hbm, scale_ref)
+    load("wo", wo_hbm, wo)
+    load("mixed", mixed_hbm, mixed_ref)
+    load("ratio", ratio_hbm, ratio_ref)
+    load("inverse", inverse_hbm, inverse_ref)
+    load("early", early_hbm, early_ref)
+    load("before", before_hbm, before)
+    load("trigs", trigs_hbm, trigs)
+    red = Reduction(stage, sums, first_in, second_in, third_in, done, core_send, core_recv, send, recv)
+
+    def note(k, value):
+        vec_ref[k : k + 1, :] += value
+
+    ready("gffn", "act")
+    greeted(everywhere)
+
+    def down_rows(y, carry):
+        turned[...] = act[:, at(y, WIDTH)].T
+        for s in range(3):
+            value = nn(turned[...], gffn_ref[:, 256 * s : 256 * s + 256]).reshape(4, 2, 4, 24, 256)
+            for side in range(2):
+                stage[s, side, y] = value[:, side]
+            red.swap(0, s, y).start()
+        return carry
+
+    lax.fori_loop(0, 4, down_rows, 0)
+    ready("wdown", "slope", "wup", "back", "vec")
+
+    def feed_back(t, carry):
+        cols = at(t, WIDTH)
+        gpre = (nt(gffn_ref[...], bufd[cols]) * slope[:, cols].astype(F32)).astype(BF16)
+        slope[:, cols] = gpre
+        vec_ref[pl.ds(9 + t, 1), :] = column(gpre.astype(F32))
+        acc_ref[...] += nt(gpre, bufu[:, cols])
+        return carry
+
+    lax.fori_loop(0, 2, feed_back, 0)
+    red.begin(0, 0)
+    lax.fori_loop(2, 3, feed_back, 0)
+    red.begin(0, 1)
+    lax.fori_loop(3, 4, feed_back, 0)
+    red.begin(0, 2)
+    load("wq", wq_hbm, bufd.at[0:WIDTH])
+    load("wk", wk_hbm, bufd.at[WIDTH : 2 * WIDTH])
+    load("wv", wv_hbm, bufd.at[2 * WIDTH : 3 * WIDTH])
+    load("x", x_hbm, bufd.at[3 * WIDTH : 3 * WIDTH + ROWS])
+    load("qk", qk_hbm, bufu.at[0:ROWS])
+    load("v", v_hbm, act.at[:, 0 : 128 * HEADS])
+    for i in range(2):
+        for c in range(2):
+            load(f"gate{i}{c}", gates_hbm.at[i, CHUNK * c : CHUNK * c + CHUNK],
+                 bufu.at[ROWS:WIDTH, pl.ds(2 * WIDTH * i + WIDTH * c, WIDTH)])
+    ready("normal", "scale", "wo")
+
+    def first_back(r, carry):
+        rows = at(r, 128)
+        normal = normal_ref[rows]
+        scale = scale_ref[rows, 0:1]
+        grad = acc_ref[rows]
+        note(4, column(grad * normal))
+        note(5, column(grad))
+        back = norm_back(grad, normal, scale, gain1[...])
+        acc_ref[rows] = back
+        low = back.astype(BF16)
+        gffn_ref[rows] = low
+        note(3, column(low.astype(F32)))
+        normal_ref[rows] = nt(low, wo[...])
+        return carry
+
+    lax.fori_loop(0, ROWS // 128, first_back, 0)
+    ready("ratio", "inverse", "qk")
+
+    def heads_back(p, carry):
+        cols = at(p, 128)
+        lane = lax.broadcasted_iota(jnp.int32, (ROWS, 128), 1)
+        left = lane < 64
+        gnum = (normal_ref[:, cols] * inverse_ref[:, cols]).astype(BF16).astype(F32)
+        product = gnum * ratio_ref[:, cols]
+        for j in range(2):
+            h = 2 * p + j
+            mine = jnp.where(left, product, 0.0) if j == 0 else jnp.where(left, 0.0, product)
+            gden = jnp.broadcast_to(-jnp.sum(mine, axis=1, keepdims=True), (ROWS, 128))
+            high = gden.astype(BF16).astype(F32)
+            ends = jnp.where(lane == 64, high, jnp.where(lane == 65, gden - high, 0.0))
+            grad = jnp.where(left, gnum if j == 0 else swap_halves(gnum), ends).astype(BF16)
+            act[:, at(HEADS + h, 128)] = grad
+            late = tn(grad[CHUNK:ROWS], bufu[CHUNK:ROWS, at(h, 128)])
+            late_ref[h] = late
+            both = late + tn(grad[0:CHUNK], bufu[0:CHUNK, at(h, 128)])
+            pay[p, 64 * j : 64 * j + 64] = both[0:64]
+            pay[p, 128 + j : 129 + j] = both[64:65] + both[65:66]
+        pay[p, 130:136] = jnp.zeros((6, 128), F32)
+        return carry
+
+    lax.fori_loop(0, PAIRS, heads_back, 0)
+    first, second, third, fourth, fifth = exchange_steps(pay, after, *scratch, True)
+    step = first()
+    red.each(red.relay, 0)
+    ready("normed", "mixed")
+    turned[...] = normed_ref[...].T
+
+    def up_columns(b, carry):
+        for s in range(3):
+            cols = pl.ds(pl.multiple_of(WIDTH * b + 256 * s, 256), 256)
+            value = nn(turned[...], slope[:, cols]).reshape(4, 4, 2, 24, 256)
+            for side in range(2):
+                stage[s, side, :, :, b] = value[:, :, side]
+            red.swap(1, s, b).start()
+        return carry
+
+    lax.fori_loop(0, 1, up_columns, 0)
+    step = second(step)
+    lax.fori_loop(1, 4, up_columns, 0)
+    red.each(red.middle, 0)
+    step = third(step)
+    ready("v", "early", "before", "trigs", "gate00", "gate01", "gate10", "gate11")
+
+    def local(p, carry):
+        attend_back_local(p, act, bufu, early_ref, before, trigs, ratio_ref, inverse_ref, slope)
+        return carry
+
+    lax.fori_loop(0, 2, local, 0)
+    red.each(red.last, 0)
+    red.begin(1, 0)
+    lax.fori_loop(2, 4, local, 0)
+    red.each(red.spread, 0)
+    red.begin(1, 1)
+    red.begin(1, 2)
+    step = fourth(step)
+    lax.fori_loop(4, 6, local, 0)
+    red.each(red.finish, 0)
+    red.sent(0)
+    axes_of = ((CORE, (1,)),) + tuple((a, DIRECT) for a in everywhere)
+    for axis, steps in axes_of:
+        size = 2 if axis == CORE else 4
+        for d in steps:
+            pl.semaphore_signal(free_sem, inc=1, device_id={axis: lax.rem(lax.axis_index(axis) + d, size)},
+                                device_id_type=MESH)
+    red.each(red.relay, 1)
+
+    def product(rhs, base, group, b0):
+        _, start, width = GROUPS[group]
+        for n in range(3):
+            value = nn(turned[...], rhs[:, base + 256 * n : base + 256 * n + 256]).reshape(4, 4, 2, 24, 256)
+            for half in range(2):
+                unit = 2 * n + half
+                for side in range(2):
+                    stage[unit % 3, side, :, :, b0 + unit // 3, :, start : start + width] = (
+                        value[:, :, side, :, 128 * half : 128 * half + 128])
+
+    turned[...] = mixed_ref[...].T
+    product(gffn_ref, 0, 2, 0)
+    ready("wq", "wk", "wv", "x")
+    turned[...] = bufd[3 * WIDTH : 3 * WIDTH + ROWS].T
+    product(slope, 0, 2, 2)
+    pl.semaphore_wait(free_sem, 10)
+    for s in range(3):
+        for b in range(4):
+            red.swap(2, s, b).start()
+    fifth(step)
+
+    def later(p, carry):
+        attend_back_later(p, act, bufu, late_ref, after, trigs, ratio_ref, inverse_ref, slope)
+        return carry
+
+    lax.fori_loop(0, 6, later, 0)
+    product(slope, WIDTH, 3, 0)
+    product(slope, 2 * WIDTH, 3, 2)
+    for s in range(3):
+        for b in range(4):
+            red.swap(3, s, b).start()
+    for i in range(3):
+        note(i, column(slope[:, WIDTH * i : WIDTH * i + WIDTH].astype(F32)))
+    start, end, vector_sent = vector_steps(vec_ref, vecs, vec_send, vec_recv)
+    start(0)
+    red.each(red.begin, 2)
+    red.each(red.middle, 1)
+    end(0)
+    start(1)
+    red.each(red.relay, 2)
+    red.each(red.begin, 3)
 
     def back(r, carry):
         rows = at(r, 128)
-        total = gone_ref[rows]
-        for i, w in enumerate((wq, wk, wv)):
-            total = total + nt(grad_ref[i, rows], w[...])
-        tokens_ref[rows] = total
-        return carry
-
-    lax.fori_loop(0, ROWS // 128, back, 0)
-
-
-def plain_call(kernel, outs, args, specs=None, scratch=(), out_specs=None):
-    vmem = pl.BlockSpec(memory_space=VMEM)
-    return pl.pallas_call(
-        kernel,
-        out_shape=[jax.ShapeDtypeStruct(shape, dtype) for shape, dtype in outs],
-        in_specs=specs or [vmem] * len(args),
-        out_specs=out_specs or [vmem] * len(outs),
-        scratch_shapes=list(scratch),
-        compiler_params=pltpu.CompilerParams(vmem_limit_bytes=LIMIT),
-    )(*args)
+        total = acc_ref[rows]
+        for i in range(3):
+            total = total + nt(slope[rows, WIDTH * i : WIDTH * i + WIDTH], bufd[WIDTH * i : WIDTH * i + WIDTH])
+        acc_ref[rows] = total
+        return carry
+
+    lax.fori_loop(0, 2, back, 0)
+    red.each(red.last, 1)
+    red.each(red.relay, 3)
+    lax.fori_loop(2, 4, back, 0)
+    tokens_copy = pltpu.make_async_copy(acc_ref, tokens_out, store_sem.at[0])
+    tokens_copy.start()
+    end(1)
+    start(2)
+    red.each(red.middle, 2)
+    red.each(red.spread, 1)
+    red.each(red.middle, 3)
+    end(2)
+    start(3)
+    red.each(red.last, 2)
+    red.each(red.last, 3)
+    red.each(red.finish, 1)
+    red.each(red.spread, 2)
+    red.each(red.spread, 3)
+    end(3)
+    vec_copy = pltpu.make_async_copy(vecs.at[4], vec_out, store_sem.at[1])
+    vec_copy.start()
+    red.each(red.finish, 2)
+    red.each(red.finish, 3)
+    done_copy = pltpu.make_async_copy(done, done_out, store_sem.at[2])
+    done_copy.start()
+    vector_sent()
+    for g in range(1, 4):
+        red.sent(g)
+    tokens_copy.wait()
+    vec_copy.wait()
+    done_copy.wait()
+
+
+def final_kernel(done, vecs, tokens, block, block_out, tokens_out, out_q, out_bq, out_k, out_bk, out_v, out_bv, out_o,
+                 out_bo, out_g1, out_s1, out_up, out_bup, out_down, out_bdown, out_g2, out_s2, sem):
+    copies = (pltpu.make_async_copy(tokens, tokens_out, sem.at[0]), pltpu.make_async_copy(block, block_out, sem.at[1]))
+    for copy in copies:
+        copy.start()
+    for s in range(3):
+        for b in range(4):
+            out_down[24 * b : 24 * b + 24, 256 * s : 256 * s + 256] = done[0, s, b]
+            out_up[:, 768 * b + 256 * s : 768 * b + 256 * s + 256] = done[1, s, b]
+            cols = slice(384 * (b % 2) + 128 * s, 384 * (b % 2) + 128 * s + 128)
+            (out_o, out_q)[b // 2][:, cols] = done[2, s, b, :, 0:128]
+            (out_k, out_v)[b // 2][:, cols] = done[2, s, b, :, 128:256]
+    seq = (lax.axis_index("seq_0") * 4 + lax.axis_index("seq_1")) * 2 + lax.axis_index(CORE)
+    values = vecs[...]
+    mine = pltpu.roll(values, lax.rem(WIDTH - 24 * seq, WIDTH), 1)
+    for k, out in enumerate((out_bq, out_bk, out_bv, out_bo, out_g1, out_s1, out_bdown, out_g2, out_s2)):
+        out[...] = mine[k, 0:24]
+    spun = pltpu.roll(values, lax.rem(WIDTH - 96 * lax.rem(seq, 8), WIDTH), 1)
+    row = lax.broadcasted_iota(jnp.int32, (16, WIDTH), 0)
+    out_bup[...] = jnp.sum(jnp.where(row == 9 + seq // 8, spun, 0.0), axis=0)[0:96]
+    for copy in copies:
+        copy.wait()
 
 
 def on_device(tokens, lengths, w_query, b_query, w_key, b_key, w_value, b_value, w_out, b_out, gain_one, shift_one,
@@ -955,27 +1033,38 @@
         compiler_params=pltpu.CompilerParams(collective_id=2, has_side_effects=True, vmem_limit_bytes=LIMIT),
     )(lengths, row(b_query), row(b_key), row(b_value), row(b_out), row(gain_one), row(shift_one), row(b_up),
       row(b_down), row(gain_two), row(shift_two), x, w_query, w_key, w_value, w_out, w_up, w_down, cot)
-    gone, gn, after_state, late, gw_down, gw_up, gw_out, vec_one = plain_call(
-        middle_kernel,
-        [wide32, heads16, packed, per_head, ((HIDDEN, WIDTH), F32), ((WIDTH, HIDDEN), F32), ((WIDTH, WIDTH), F32), vector],
-        [qk, ratio, inverse, mixed, normal, scale, normed, act, slope, back, gffn, w_out, w_up, row(gain_one), w_down],
-        scratch=[VMEM(*wide16), VMEM(*wide32),
-            VMEM((2, TILE, WIDTH), F32), VMEM((2, WIDTH, TILE), F32), pltpu.SemaphoreType.DMA((2, 2))],
-        out_specs=[vmem] * 4 + [anywhere, anywhere, vmem, vmem])
-    after = exchange(after_state, True)
-    tokens_grad, gw_q, gw_k, gw_v, vec_two = plain_call(
-        last_kernel,
-        [wide32] + [((WIDTH, WIDTH), F32)] * 3 + [vector],
-        [x, qk, v, gn, early, late, before, after, trigs, gates, gone, w_query, w_key, w_value],
-        scratch=[VMEM((3, ROWS, WIDTH), BF16)])
-    sum_down, sum_up, sum_out, sum_query, sum_key, sum_value, sums = reduce_grads(
-        gw_down, gw_up, gw_out, gw_q, gw_k, gw_v, vec + vec_one + vec_two)
-    small = lax.dynamic_slice(sums, (0, 24 * seq), (9, 24))
-    wide = lax.dynamic_slice(sums[9:15, :TILE].reshape(-1), (96 * seq,), (96,))
-    return (
-        block[None], tokens_grad[None], sum_query, small[0], sum_key, small[1], sum_value, small[2],
-        sum_out, small[3], small[4], small[5], sum_up, wide, sum_down, small[6], small[7], small[8],
-    )
+    anywhere_of = [qk, v, gates, trigs, early, before, ratio, inverse, mixed, normal, scale, normed, act, slope, back, gffn,
+                   vec, x, w_query, w_key, w_value, w_out, w_up, w_down]
+    tokens_grad, done, sums = pl.pallas_call(
+        back_kernel,
+        out_shape=[jax.ShapeDtypeStruct(*wide32), jax.ShapeDtypeStruct((3, 3, 4, 24, 256), F32),
+                   jax.ShapeDtypeStruct(*vector)],
+        in_specs=[vmem] + [anywhere] * len(anywhere_of),
+        out_specs=[anywhere] * 3,
+        scratch_shapes=[VMEM(*shape) for shape in (
+            ((2, ROWS, 128), F32), per_head, packed, wide32, wide32, wide16, wide32, ((ROWS, 128), F32), wide16,
+            long16, long16, wide32, wide16, vector, square, ((WIDTH, HIDDEN), BF16), ((HIDDEN, WIDTH), BF16),
+            per_head, packed, packed, ((WIDTH, ROWS), BF16),
+            ((3, 2, 4, 4, 4, 24, 256), F32), ((2, 3, 4, 4, 4, 24, 256), F32), ((2, 3, 3, 4, 4, 24, 256), F32),
+            ((2, 3, 3, 4, 24, 256), F32), ((2, 3, 3, 24, 256), F32), ((3, 3, 4, 24, 256), F32), ((15, 16, WIDTH), F32))]
+        + [pltpu.SemaphoreType.DMA((32,)), pltpu.SemaphoreType.DMA((3,)), pltpu.SemaphoreType.DMA((4, 3, 4)),
+           pltpu.SemaphoreType.DMA((4, 3, 4)), pltpu.SemaphoreType.DMA((4, 3, 15)), pltpu.SemaphoreType.DMA((4, 3, 15)),
+           pltpu.SemaphoreType.DMA((10,)), pltpu.SemaphoreType.DMA((10,)), pltpu.SemaphoreType.REGULAR]
+        + EXCHANGE_SCRATCH,
+        compiler_params=pltpu.CompilerParams(collective_id=1, has_side_effects=True, vmem_limit_bytes=BACK_LIMIT),
+    )(row(gain_one), *anywhere_of)
+    out = jax.ShapeDtypeStruct
+    square_share, vector_share = out((24, WIDTH), F32), out((24,), F32)
+    results = pl.pallas_call(
+        final_kernel,
+        out_shape=[out(*wide16), out(*wide32)] + [square_share, vector_share] * 4 + [vector_share] * 2
+        + [out((24, HIDDEN), F32), out((96,), F32), out((96, WIDTH), F32)] + [vector_share] * 3,
+        in_specs=[vmem, vmem, anywhere, anywhere],
+        out_specs=[anywhere] * 2 + [vmem] * 16,
+        scratch_shapes=[pltpu.SemaphoreType.DMA((2,))],
+        compiler_params=pltpu.CompilerParams(vmem_limit_bytes=32 * 2**20),
+    )(done, sums, tokens_grad, block)
+    return (results[0][None], results[1][None], *results[2:])
 
 
 def solution(mesh):

time: 241 us -> 177 us (0.73)
  Pallas kernels: 218 us -> 160 us
  local copies, waits for them, and re-layouts: 19.3 us -> 14.8 us
    pallas_call x4 -> x2, Pallas kernels: 168 us -> 111 us  [the longest x1 109 us: on_device(): pl.pallas_call(back_kernel, out_shape=[jax.ShapeDtypeStruct(*wide32), jax...]
    unnamed x25 -> x8, local copies, waits for them, and re-layouts: 4.88 us -> 3.37 us
where the time goes in v2:
time: 177 us
  Pallas kernels  160 us (90%)
  local copies, waits for them, and re-layouts  14.8 us (8%)
    pallas_call x1, Pallas kernels, on_device(): pl.pallas_call(back_kernel, out_shape=[jax.ShapeDtypeStruct(*wide32), jax...  109 us
    pallas_call x1, Pallas kernels, on_device(): pl.pallas_call(front_kernel, out_shape=[jax.ShapeDtypeStruct(*shape) for...  49.3 us
    reshape x9, local copies, waits for them, and re-layouts, row(): return v.reshape(1, -1)  11.4 us

profile of v2, /device:TPU:0, one launch (start us, length us, event | category | flops | bytes accessed | tf_op | source)
XLA Modules:
  0.0 176.7 jit_solution(16148777515407481140)
XLA Ops:
  1.3 1.3 reshape.67.gain1
  2.6 1.3 reshape.68.bq
  3.8 1.3 reshape.69.bk
  5.1 1.3 reshape.70.bv
  6.4 1.3 reshape.71.bo
  7.6 1.3 reshape.72.shift1
  8.9 1.3 reshape.74.bdown
  10.2 1.3 reshape.75.gain2
  11.4 1.3 reshape.76.shift2
  12.7 49.3 %shard_map.322 = (bf16[512,3072]{1,0:T(8,128)(2,1)}, bf16[512,1536]{1,0:T(8,128)(2,1)}, bf16[2,512,768]{2,1,0:T(8,128)(2,1)}, f32[2,512,128]{2,1,0:T(8,128)}, f3...) custom-call(s32[1]{0:T(128)S(6)} %copy.37.len_ref, ...), custom_call_target="tpu_custom_call" | custom-call | tf_op jit(solution)/shard_map/pallas_call | solution.py:1024
  62.1 0.0 copy-start.2
  62.1 108.7 %shard_map.323 = (f32[512,768]{1,0:T(8,128)}, f32[3,3,4,24,256]{4,3,2,1,0:T(8,128)}, f32[16,768]{1,0:T(8,128)}) custom-call(f32[1,768]{1,0:T(1,128)} %reshape.67.gain1, bf16[512,3072]{1,0:T(8,128)(2,1)} %get-tuple-element.57.qk_hbm, bf16[512,1536]{1,0:T(8,128)(2,1)} %get-tuple-element.58.v_hbm, bf16[2,512,768]{2,1,0:T(8,128)(2,1)} %get-tuple-element.59.gates_hbm, ...), custom_call_target="tpu_custom_call" | custom-call | tf_op jit(solution)/shard_map/pallas_call | solution.py:1038
  170.8 0.0 copy-done.2
  170.8 0.0 copy-start
  170.8 1.4 copy-done
  172.2 0.0 copy-start.1
  172.2 1.2 copy-done.1
  173.4 0.0 copy-start.3
  173.4 0.8 copy-done.3
  174.2 2.4 %shard_map.324 = (bf16[512,768]{1,0:T(8,128)(2,1)}, f32[512,768]{1,0:T(8,128)}, f32[24,768]{1,0:T(8,128)}, f32[24]{0:T(128)}, f32[24,768]{1,0:T(8,128)}, /*index...) custom-call(f32[3,3,4,24,256]{4,3,2,1,0:T(8,128)S(1)} %copy-done.1, ...), custom_call_target="tpu_custom_call" | custom-call | tf_op jit(solution)/shard_map/pallas_call | solution.py:1058
Async XLA Ops:
  62.1 108.7 %copy-start.2 = (bf16[512,768]{1,0:T(8,128)(2,1)S(1)}, bf16[512,768]{1,0:T(8,128)(2,1)}, u32[]{:S(2)}) copy-start(bf16[512,768]{1,0:T(8,128)(2,1)} %get-tuple-element.77.block) | copy-start | bytes 2359300
  170.8 1.4 copy-start
  172.2 1.2 copy-start.1
  173.4 0.8 copy-start.3
